TPU v7x, 128 devices: a whole 4x4x4 slice. The times are simulated.
128 devices in a mesh: group: 2 (over z_hi), replica: 64 (over y, z_lo, x, core).
Axes of the slice: x: 4, y: 4, z: 4 (z_hi: 2, z_lo: 2; z = z_hi * 2 + z_lo), core: 2. Of those that a mesh axis runs over, the one named last changes fastest.
Arguments:
- tokens: bfloat16 [16384, 2560], P(('group', 'replica')), may hold values from -6 to 6
- entry_gain: bfloat16 [2560], P(('group', 'replica')), may hold values from 0.25 to 1.75
- query_down: bfloat16 [2560, 768], P(('group', 'replica')), may hold values from -0.125 to 0.125
- query_gain: bfloat16 [768], P(('group', 'replica')), may hold values from 0.25 to 1.75
- query_up: bfloat16 [768, 3840], P(('group', 'replica')), may hold values from -0.21875 to 0.21875
- latent_down: bfloat16 [2560, 288], P(('group', 'replica')), may hold values from -0.125 to 0.125
- latent_gain: bfloat16 [256], P(('group', 'replica')), may hold values from 0.25 to 1.75
- latent_up: bfloat16 [256, 5120], P(('group', 'replica')), may hold values from -0.375 to 0.375
- output_weight: bfloat16 [2560, 2560], P(('group', 'replica')), may hold values from -4 to 4
- ffn_gain: bfloat16 [2560], P(('group', 'replica')), may hold values from 0.25 to 1.75
- gate_weight: bfloat16 [2560, 6400], P(('group', 'replica')), may hold values from -0.125 to 0.125
- up_weight: bfloat16 [2560, 6400], P(('group', 'replica')), may hold values from -0.125 to 0.125
- down_weight: bfloat16 [6400, 2560], P(('group', 'replica')), may hold values from -0.625 to 0.625
- cotangent: bfloat16 [16384, 2560], P(('group', 'replica')), may hold values from -6 to 6
Outputs:
- block_out: bfloat16 [16384, 2560], P(('group', 'replica'))
- tokens_grad: float32 [16384, 2560], P(('group', 'replica'))
- entry_gain_grad: float32 [2560], P(('group', 'replica'))
- query_down_grad: float32 [2560, 768], P(('group', 'replica'))
- query_gain_grad: float32 [768], P(('group', 'replica'))
- query_up_grad: float32 [768, 3840], P(('group', 'replica'))
- latent_down_grad: float32 [2560, 288], P(('group', 'replica'))
- latent_gain_grad: float32 [256], P(('group', 'replica'))
- latent_up_grad: float32 [256, 5120], P(('group', 'replica'))
- output_weight_grad: float32 [2560, 2560], P(('group', 'replica'))
- ffn_gain_grad: float32 [2560], P(('group', 'replica'))
- gate_weight_grad: float32 [2560, 6400], P(('group', 'replica'))
- up_weight_grad: float32 [2560, 6400], P(('group', 'replica'))
- down_weight_grad: float32 [6400, 2560], P(('group', 'replica'))
All inputs are finite; a program needn't handle non-finite values.
Results may differ from a plain program's by a relative error of at most 0.025.
Values may be sent and summed in bfloat16 or wider, within the bound.
No kernel may reach another device: no remote copies, remote signals or barrier semaphores. Data moves between devices by JAX's collectives and lax.ppermute only.
A program may use at most 768 MiB of HBM per device.

v0:
```python
import math

import jax
import jax.numpy as jnp
from jax import lax
from jax.sharding import PartitionSpec as P

KVR = 256
HEADS = 40
NOPE = 64
ROPE = 32
VDIM = 64
SEQ_LEN = 128


EPS = 1e-05
RESIDUAL = 1.4 / math.sqrt(62.0)
NEGATIVE = -1e30


def angles(count):
    place = (lax.iota(jnp.int32, count) % SEQ_LEN).astype(jnp.float32)
    freqs = 10000.0 ** (-2.0 * lax.iota(jnp.float32, ROPE // 2) / ROPE)
    turn = place[:, None] * freqs[None, :]
    return (jnp.cos(turn), jnp.sin(turn))


def rotate(pair, cosine, sine):
    half = pair.shape[-1] // 2
    first, second = (pair[..., :half], pair[..., half:])
    return jnp.concatenate(
        [first * cosine - second * sine, first * sine + second * cosine], axis=-1
    )


def unrotate(pair, cosine, sine):
    half = pair.shape[-1] // 2
    first, second = (pair[..., :half], pair[..., half:])
    return jnp.concatenate(
        [first * cosine + second * sine, second * cosine - first * sine], axis=-1
    )


def rms_apply(value, gain):
    factor = lax.rsqrt(jnp.mean(value * value, axis=-1, keepdims=True) + EPS)
    return (value * factor * gain, factor)


def norm_back(value, factor, gain, incoming):
    scaled = incoming * gain
    gain_grad = jnp.sum(incoming * value * factor, axis=0)
    value_grad = factor * scaled - value * factor**3 * jnp.mean(
        scaled * value, axis=-1, keepdims=True
    )
    return (value_grad, gain_grad)


def masked_scores(queries, keys):
    scores = jnp.einsum("shd,thd->hst", queries, keys, preferred_element_type=jnp.float32) * (
        NOPE + ROPE
    ) ** (-0.5)
    length = queries.shape[0]
    rows = lax.broadcasted_iota(jnp.int32, (length, length), 0)
    cols = lax.broadcasted_iota(jnp.int32, (length, length), 1)
    return jnp.where(rows >= cols, scores, NEGATIVE)


def attend(blocks):
    queries, keys, values = blocks
    scores = masked_scores(queries, keys)
    top = jnp.max(scores, axis=-1, keepdims=True)
    expo = jnp.exp(scores - top)
    total = jnp.sum(expo, axis=-1, keepdims=True)
    probs_low = (expo / total).astype(jnp.bfloat16)
    attended = jnp.einsum("hst,thd->shd", probs_low, values, preferred_element_type=jnp.float32)
    return (attended.astype(jnp.bfloat16), top + jnp.log(total))


def attend_back(blocks):
    queries, keys, values, attended_grad, logsum = blocks
    probs = jnp.exp(masked_scores(queries, keys) - logsum)
    probs_low = probs.astype(jnp.bfloat16)
    probs_grad = jnp.einsum(
        "shd,thd->hst", attended_grad, values, preferred_element_type=jnp.float32
    )
    inner = jnp.sum(probs * probs_grad, axis=-1, keepdims=True)
    scores_grad = (probs * (probs_grad - inner)).astype(jnp.bfloat16)
    scale = (NOPE + ROPE) ** (-0.5)
    query_grad = (
        jnp.einsum("hst,thd->shd", scores_grad, keys, preferred_element_type=jnp.float32) * scale
    )
    key_grad = (
        jnp.einsum("hst,shd->thd", scores_grad, queries, preferred_element_type=jnp.float32) * scale
    )
    value_grad = jnp.einsum(
        "hst,shd->thd", probs_low, attended_grad, preferred_element_type=jnp.float32
    )
    return (query_grad, key_grad, value_grad)


def outer(left, right):
    return lax.dot_general(
        left, right, (((0,), (0,)), ((), ())), preferred_element_type=jnp.float32
    )


def back_product(left, matrix):
    return lax.dot_general(
        left, matrix, (((1,), (1,)), ((), ())), preferred_element_type=jnp.float32
    )


def on_device(
    tokens,
    entry_gain,
    query_down,
    query_gain,
    query_up,
    latent_down,
    latent_gain,
    latent_up,
    output_weight,
    ffn_gain,
    gate_weight,
    up_weight,
    down_weight,
    cotangent,
):
    attn_whole = (
        lax.all_gather(entry_gain, ("group", "replica"), axis=0, tiled=True),
        lax.all_gather(query_down, ("group", "replica"), axis=0, tiled=True),
        lax.all_gather(query_gain, ("group", "replica"), axis=0, tiled=True),
        lax.all_gather(query_up, ("group", "replica"), axis=0, tiled=True),
        lax.all_gather(latent_down, ("group", "replica"), axis=0, tiled=True),
        lax.all_gather(latent_gain, ("group", "replica"), axis=0, tiled=True),
        lax.all_gather(latent_up, ("group", "replica"), axis=0, tiled=True),
        lax.all_gather(output_weight, ("group", "replica"), axis=0, tiled=True),
    )
    (
        gain_first,
        down_query,
        gain_query,
        up_query,
        down_latent,
        gain_latent,
        up_latent,
        out_matrix,
    ) = attn_whole
    count = tokens.shape[0]
    seqs = count // SEQ_LEN
    cosine, sine = angles(count)
    inputs = tokens.astype(jnp.float32)
    normed_full, entry_factor = rms_apply(inputs, gain_first.astype(jnp.float32))
    normed = normed_full.astype(jnp.bfloat16)
    query_latent = jnp.dot(normed, down_query, preferred_element_type=jnp.float32)
    query_normed_full, query_factor = rms_apply(query_latent, gain_query.astype(jnp.float32))
    query_normed = query_normed_full.astype(jnp.bfloat16)
    query_full = jnp.dot(query_normed, up_query, preferred_element_type=jnp.float32).reshape(
        count, HEADS, NOPE + ROPE
    )
    queries = jnp.concatenate(
        [
            query_full[..., :NOPE],
            rotate(query_full[..., NOPE:], cosine[:, None, :], sine[:, None, :]),
        ],
        axis=-1,
    ).astype(jnp.bfloat16)
    latent_full = jnp.dot(normed, down_latent, preferred_element_type=jnp.float32)
    latent_part = latent_full[:, :KVR]
    latent_normed_full, latent_factor = rms_apply(latent_part, gain_latent.astype(jnp.float32))
    latent_normed = latent_normed_full.astype(jnp.bfloat16)
    key_value = jnp.dot(latent_normed, up_latent, preferred_element_type=jnp.float32).reshape(
        count, HEADS, NOPE + VDIM
    )
    key_rope = rotate(latent_full[:, KVR:], cosine, sine)
    keys = jnp.concatenate(
        [key_value[..., :NOPE], jnp.broadcast_to(key_rope[:, None, :], (count, HEADS, ROPE))],
        axis=-1,
    ).astype(jnp.bfloat16)
    values = key_value[..., NOPE:].astype(jnp.bfloat16)
    query_seqs = queries.reshape(seqs, SEQ_LEN, HEADS, NOPE + ROPE)
    key_seqs = keys.reshape(seqs, SEQ_LEN, HEADS, NOPE + ROPE)
    value_seqs = values.reshape(seqs, SEQ_LEN, HEADS, VDIM)
    attended_seqs, logsum = lax.map(attend, (query_seqs, key_seqs, value_seqs))
    attended = attended_seqs.reshape(count, HEADS * VDIM)
    branch = jnp.dot(attended, out_matrix, preferred_element_type=jnp.float32)
    middle = inputs + RESIDUAL * branch
    ffn_whole = (
        lax.all_gather(ffn_gain, ("group", "replica"), axis=0, tiled=True),
        lax.all_gather(gate_weight, ("group", "replica"), axis=0, tiled=True),
        lax.all_gather(up_weight, ("group", "replica"), axis=0, tiled=True),
        lax.all_gather(down_weight, ("group", "replica"), axis=0, tiled=True),
    )
    gain_ffn, gate_matrix, up_matrix, down_matrix = ffn_whole
    ffn_normed_full, ffn_factor = rms_apply(middle, gain_ffn.astype(jnp.float32))
    ffn_normed = ffn_normed_full.astype(jnp.bfloat16)
    gate = jnp.dot(ffn_normed, gate_matrix, preferred_element_type=jnp.float32)
    upper = jnp.dot(ffn_normed, up_matrix, preferred_element_type=jnp.float32)
    sigma = jax.nn.sigmoid(gate)
    swish = gate * sigma
    hidden = (swish * upper).astype(jnp.bfloat16)
    ffn_branch = jnp.dot(hidden, down_matrix, preferred_element_type=jnp.float32)
    block_out = (middle + RESIDUAL * ffn_branch).astype(jnp.bfloat16)
    ffn_again = (
        lax.all_gather(ffn_gain, ("group", "replica"), axis=0, tiled=True),
        lax.all_gather(gate_weight, ("group", "replica"), axis=0, tiled=True),
        lax.all_gather(up_weight, ("group", "replica"), axis=0, tiled=True),
        lax.all_gather(down_weight, ("group", "replica"), axis=0, tiled=True),
    )
    gain_ffn, gate_matrix, up_matrix, down_matrix = ffn_again
    incoming = cotangent.astype(jnp.float32)
    ffn_branch_grad = (RESIDUAL * incoming).astype(jnp.bfloat16)
    down_grad = outer(hidden, ffn_branch_grad)
    total_down = lax.psum_scatter(down_grad, ("group", "replica"), scatter_dimension=0, tiled=True)
    hidden_grad = back_product(ffn_branch_grad, down_matrix)
    gate_grad = (hidden_grad * upper * (sigma + gate * sigma * (1.0 - sigma))).astype(jnp.bfloat16)
    upper_grad = (hidden_grad * swish).astype(jnp.bfloat16)
    gate_matrix_grad = outer(ffn_normed, gate_grad)
    up_matrix_grad = outer(ffn_normed, upper_grad)
    ffn_normed_grad = back_product(gate_grad, gate_matrix) + back_product(upper_grad, up_matrix)
    middle_part, gain_ffn_grad = norm_back(
        middle, ffn_factor, gain_ffn.astype(jnp.float32), ffn_normed_grad
    )
    middle_grad = incoming + middle_part
    total_fgain, total_gate, total_up = (
        lax.psum_scatter(gain_ffn_grad, ("group", "replica"), scatter_dimension=0, tiled=True),
        lax.psum_scatter(gate_matrix_grad, ("group", "replica"), scatter_dimension=0, tiled=True),
        lax.psum_scatter(up_matrix_grad, ("group", "replica"), scatter_dimension=0, tiled=True),
    )
    attn_again = (
        lax.all_gather(entry_gain, ("group", "replica"), axis=0, tiled=True),
        lax.all_gather(query_down, ("group", "replica"), axis=0, tiled=True),
        lax.all_gather(query_gain, ("group", "replica"), axis=0, tiled=True),
        lax.all_gather(query_up, ("group", "replica"), axis=0, tiled=True),
        lax.all_gather(latent_down, ("group", "replica"), axis=0, tiled=True),
        lax.all_gather(latent_gain, ("group", "replica"), axis=0, tiled=True),
        lax.all_gather(latent_up, ("group", "replica"), axis=0, tiled=True),
        lax.all_gather(output_weight, ("group", "replica"), axis=0, tiled=True),
    )
    (
        gain_first,
        down_query,
        gain_query,
        up_query,
        down_latent,
        gain_latent,
        up_latent,
        out_matrix,
    ) = attn_again
    branch_grad = (RESIDUAL * middle_grad).astype(jnp.bfloat16)
    out_grad = outer(attended, branch_grad)
    attended_grad = back_product(branch_grad, out_matrix).astype(jnp.bfloat16)
    grad_seqs = attended_grad.reshape(seqs, SEQ_LEN, HEADS, VDIM)
    query_grad, key_grad, value_grad = lax.map(
        attend_back, (query_seqs, key_seqs, value_seqs, grad_seqs, logsum)
    )
    query_grad = query_grad.reshape(count, HEADS, NOPE + ROPE)
    key_grad = key_grad.reshape(count, HEADS, NOPE + ROPE)
    value_grad = value_grad.reshape(count, HEADS, VDIM)
    query_full_grad = (
        jnp.concatenate(
            [
                query_grad[..., :NOPE],
                unrotate(query_grad[..., NOPE:], cosine[:, None, :], sine[:, None, :]),
            ],
            axis=-1,
        )
        .astype(jnp.bfloat16)
        .reshape(count, HEADS * (NOPE + ROPE))
    )
    up_query_grad = outer(query_normed, query_full_grad)
    query_normed_grad = back_product(query_full_grad, up_query)
    query_latent_grad, gain_query_grad = norm_back(
        query_latent, query_factor, gain_query.astype(jnp.float32), query_normed_grad
    )
    query_latent_low = query_latent_grad.astype(jnp.bfloat16)
    down_query_grad = outer(normed, query_latent_low)
    key_value_grad = (
        jnp.concatenate([key_grad[..., :NOPE], value_grad], axis=-1)
        .astype(jnp.bfloat16)
        .reshape(count, HEADS * (NOPE + VDIM))
    )
    up_latent_grad = outer(latent_normed, key_value_grad)
    latent_normed_grad = back_product(key_value_grad, up_latent)
    latent_part_grad, gain_latent_grad = norm_back(
        latent_part, latent_factor, gain_latent.astype(jnp.float32), latent_normed_grad
    )
    rope_grad = unrotate(jnp.sum(key_grad[..., NOPE:], axis=1), cosine, sine)
    latent_full_grad = jnp.concatenate([latent_part_grad, rope_grad], axis=-1).astype(jnp.bfloat16)
    down_latent_grad = outer(normed, latent_full_grad)
    normed_grad = back_product(query_latent_low, down_query) + back_product(
        latent_full_grad, down_latent
    )
    entry_grad, gain_first_grad = norm_back(
        inputs, entry_factor, gain_first.astype(jnp.float32), normed_grad
    )
    tokens_grad = middle_grad + entry_grad
    attn_sums = (
        lax.psum_scatter(gain_first_grad, ("group", "replica"), scatter_dimension=0, tiled=True),
        lax.psum_scatter(down_query_grad, ("group", "replica"), scatter_dimension=0, tiled=True),
        lax.psum_scatter(gain_query_grad, ("group", "replica"), scatter_dimension=0, tiled=True),
        lax.psum_scatter(up_query_grad, ("group", "replica"), scatter_dimension=0, tiled=True),
        lax.psum_scatter(down_latent_grad, ("group", "replica"), scatter_dimension=0, tiled=True),
        lax.psum_scatter(gain_latent_grad, ("group", "replica"), scatter_dimension=0, tiled=True),
        lax.psum_scatter(up_latent_grad, ("group", "replica"), scatter_dimension=0, tiled=True),
        lax.psum_scatter(out_grad, ("group", "replica"), scatter_dimension=0, tiled=True),
    )
    (
        total_entry,
        total_qdown,
        total_qgain,
        total_qup,
        total_ldown,
        total_lgain,
        total_lup,
        total_out,
    ) = attn_sums
    return (
        block_out,
        tokens_grad,
        total_entry,
        total_qdown,
        total_qgain,
        total_qup,
        total_ldown,
        total_lgain,
        total_lup,
        total_out,
        total_fgain,
        total_gate,
        total_up,
        total_down,
    )


def solution(mesh):
    placed = (
        P(("group", "replica"), None),
        P(("group", "replica")),
        P(("group", "replica"), None),
        P(("group", "replica")),
        P(("group", "replica"), None),
        P(("group", "replica"), None),
        P(("group", "replica")),
        P(("group", "replica"), None),
        P(("group", "replica"), None),
        P(("group", "replica")),
        P(("group", "replica"), None),
        P(("group", "replica"), None),
        P(("group", "replica"), None),
        P(("group", "replica"), None),
    )
    return jax.shard_map(
        on_device,
        mesh=mesh,
        in_specs=placed,
        out_specs=(
            P(("group", "replica"), None),
            P(("group", "replica"), None),
            P(("group", "replica")),
            P(("group", "replica"), None),
            P(("group", "replica")),
            P(("group", "replica"), None),
            P(("group", "replica"), None),
            P(("group", "replica")),
            P(("group", "replica"), None),
            P(("group", "replica"), None),
            P(("group", "replica")),
            P(("group", "replica"), None),
            P(("group", "replica"), None),
            P(("group", "replica"), None),
        ),
        check_vma=False,
    )
```

profile of v0, /device:TPU:31, one launch (start us, length us, event | category | flops | bytes accessed | tf_op | source)
XLA Modules:
  0.0 4342.6 jit_solution(16194625670095113402)
XLA Ops:
  16.1 65.7 %all-reduce.22 = (bf16[2560]{0:T(1024)(128)(2,1)S(1)}, bf16[256]{0:T(256)(128)(2,1)S(1)}, bf16[768]{0:T(1024)(128)(2,1)S(1)}, bf16[2560]{0:T(1024)(128)(2,1)S(1)}) all-reduce(bf16[2560]{0:T(1024)(128)(2,1)S(1)} %dynamic-update-slice, bf16[256]{0:T(256)(128)(2,1)S(1)} %dynamic-update-slice.1, ...), channel_id=1, replica_groups=mesh['group'=2,'replica'=64] {'group','replica'}, use_global_device_ids=true, to_apply=%add | all-reduce | flops 6144 | bytes 24576
  83.9 121.5 %all-gather.17.cloned.1.call-done = bf16[128,20,288]{2,1,0:T(8,128)(2,1)} async-done(((bf16[1,20,288]{2,1,0:T(8,128)(2,1)}), bf16[128,20,288]{2,1,0:T(8,128)(2,1)}) %all-gather.17.cloned.1.call-update) | async-done | bytes 1474576 | tf_op jit(solution)/shard_map/all_gather | solution.py:134
  209.9 192.0 %all-gather.19.cloned.1.call-done = bf16[128,2,5120]{2,1,0:T(2,128)(2,1)} async-done(((bf16[1,2,5120]{2,1,0:T(2,128)(2,1)}), bf16[128,2,5120]{2,1,0:T(2,128)(2,1)}) %all-gather.19.cloned.1.call-update) | async-done | bytes 2621456 | tf_op jit(solution)/shard_map/all_gather | solution.py:136
  412.7 188.9 %all-gather.21.cloned.1.call-done = bf16[128,20,768]{2,1,0:T(8,128)(2,1)} async-done(((bf16[1,20,768]{2,1,0:T(8,128)(2,1)}), bf16[128,20,768]{2,1,0:T(8,128)(2,1)}) %all-gather.21.cloned.1.call-update) | async-done | bytes 3932176 | tf_op jit(solution)/shard_map/all_gather | solution.py:131
  612.0 192.6 %all-gather.23.cloned.1.call-done = bf16[128,6,3840]{2,1,0:T(8,128)(2,1)} async-done(((bf16[1,6,3840]{2,1,0:T(8,128)(2,1)}), bf16[128,6,3840]{2,1,0:T(8,128)(2,1)}) %all-gather.23.cloned.1.call-update) | async-done | bytes 5898256 | tf_op jit(solution)/shard_map/all_gather | solution.py:133
  823.9 193.8 %all-gather.25.cloned.1.call-done = bf16[128,20,2560]{2,1,0:T(8,128)(2,1)} async-done(((bf16[1,20,2560]{2,1,0:T(8,128)(2,1)}), bf16[128,20,2560]{2,1,0:T(8,128)(2,1)}) %all-gather.25.cloned.1.call-update) | async-done | bytes 13107216 | tf_op jit(solution)/shard_map/all_gather | solution.py:137
  1043.8 217.9 %all-gather.27.cloned.1.call-done = bf16[128,20,6400]{2,1,0:T(8,128)(2,1)} async-done(((bf16[1,20,6400]{2,1,0:T(8,128)(2,1)}), bf16[128,20,6400]{2,1,0:T(8,128)(2,1)}) %all-gather.27.cloned.1.call-update) | async-done | bytes 32768016 | tf_op jit(solution)/shard_map/all_gather | solution.py:190
  1261.7 47.5 %reshape.236 = bf16[2560,6400]{1,0:T(8,128)(2,1)} reshape(bf16[128,20,6400]{2,1,0:T(8,128)(2,1)} %all-gather.27.cloned.1.call-done) | data formatting | bytes 65536000
  1309.2 196.2 %all-gather.29.cloned.1.call-done = bf16[128,20,6400]{2,1,0:T(8,128)(2,1)} async-done(((bf16[1,20,6400]{2,1,0:T(8,128)(2,1)}), bf16[128,20,6400]{2,1,0:T(8,128)(2,1)}) %all-gather.29.cloned.1.call-update) | async-done | bytes 32768016 | tf_op jit(solution)/shard_map/all_gather | solution.py:191
  1505.4 47.5 %reshape.238 = bf16[2560,6400]{1,0:T(8,128)(2,1)} reshape(bf16[128,20,6400]{2,1,0:T(8,128)(2,1)} %all-gather.29.cloned.1.call-done) | data formatting | bytes 65536000
  1583.2 161.8 %all-gather.31.cloned.1.call-done = bf16[128,50,2560]{2,1,0:T(8,128)(2,1)} async-done(((bf16[1,50,2560]{2,1,0:T(8,128)(2,1)}), bf16[128,50,2560]{2,1,0:T(8,128)(2,1)}) %all-gather.31.cloned.1.call-update) | async-done | bytes 32768016 | tf_op jit(solution)/shard_map/all_gather | solution.py:192
  1745.0 37.6 reshape.240
  1919.3 403.9 %fusion.68 = (f32[24,768]{1,0:T(8,128)}, f32[8,3840]{1,0:T(8,128)}, f32[24,2560]{1,0:T(8,128)}) fusion(f32[2560,768]{1,0:T(8,128)} %fusion.62, f32[768,3840]{1,0:T(8,128)} %fusion.59, f32[2560,2560]{1,0:T(8,128)} %fusion.32), kind=kCustom, calls=%all-reduce-scatter.4 | all-reduce-scatter fusion | flops 14155778 | bytes 46317568
  2377.2 49.6 %collective-permute-start.15 = (f32[24,768]{1,0:T(8,128)}, f32[24,768]{1,0:T(8,128)S(1)}, u32[]{:S(2)}, u32[]{:S(2)}) collective-permute-start(f32[24,768]{1,0:T(8,128)} %get-tuple-element.81), channel_id=1, source_target_pairs={{0,16},{1,17},{2,18},{3,19},{4,20},{5,21},{6,22},{7,23},{8,24},{9,... | collective-permute-start | bytes 221192
  2735.7 839.0 %fusion.3 = f32[64,2560]{1,0:T(8,128)S(1)} fusion(f32[6400,2560]{1,0:T(8,128)} %fusion.25), kind=kCustom, calls=%all-reduce-scatter.3 | all-reduce-scatter fusion | flops 20971520 | bytes 66191360
  3663.0 43.1 collective-permute-start.100
  3706.1 35.5 collective-permute-start.99
  3749.8 31.2 collective-permute-done.99
  3815.8 33.0 collective-permute-start.91
  3911.7 46.7 %collective-permute-start.86 = (f32[64,2560]{1,0:T(8,128)S(1)}, f32[64,2560]{1,0:T(8,128)}, u32[]{:S(2)}, u32[]{:S(2)}) collective-permute-start(f32[64,2560]{1,0:T(8,128)S(1)} %fusion.3), channel_id=1, source_target_pairs={{0,11},{1,12},{2,13},{3,14},{4,15},{5,16},{6,17},{7,18},{8,19},{9,... | collective-permute-start | bytes 1966088
  3961.8 106.6 %all-reduce.20 = (f32[2560]{0:T(1024)S(1)}, f32[768]{0:T(1024)S(1)}, f32[256]{0:T(256)S(1)}, f32[2560]{0:T(1024)S(1)}) all-reduce(f32[2560]{0:T(1024)S(1)} %get-tuple-element.61, f32[768]{0:T(1024)S(1)} %get-tuple-element.63, f32[256]{0:T(256)S(1)} %get-tuple-element.65, ...), channel_id=2, replica_groups=mesh['group'=2,'replica'=64] {'group','replica'}, use_global_device_ids=true, to_apply=%region_13.14.clone | all-reduce | flops 6144 | bytes 49152
  4106.1 57.0 %concatenate.30 = f32[262,3840]{1,0:T(8,128)} concatenate(f32[6,3840]{1,0:T(8,128)S(1)} %copy-done.69, f32[8,3840]{1,0:T(8,128)} %copy-done.70, f32[8,3840]{1,0:T(8,128)} %copy-done.71, f32[8,3840]{1,0:T(8,128)} %copy-done.72, f32[8,3840]{1,0:T(8,128)} %copy-done.73, f32[8,3840]{1,0:T(8,128)} %copy-done.74, f32[8,3840]{1,0:T(8,128)} %copy-done.75, f32[8,3840]{1,0:T(8,128)} %copy-done.76, ...), dimensions={0} | concatenate | bytes 8048640
  4182.2 40.2 concatenate.31
  4231.0 95.6 %concatenate.32 = f32[1842,2560]{1,0:T(8,128)} concatenate(f32[50,2560]{1,0:T(8,128)} %copy-done.49, f32[64,2560]{1,0:T(8,128)S(1)} %copy-done.46, f32[64,2560]{1,0:T(8,128)S(1)} %copy-done.48, f32[64,2560]{1,0:T(8,128)} %collective-permute-done.100, f32[64,2560]{1,0:T(8,128)} %collective-permute-done.99, f32[64,2560]{1,0:T(8,128)} %collective-permute-done.98, ...), dimensions={0} | concatenate | bytes 37724160
  (634 shorter events, 880.2 us)
Async XLA Ops:
  7.2 198.3 %all-gather.17.cloned.1.call-start = ((), (), s32[]{:S(2)}) async-start(), calls=%async_computation | async-start | bytes 2377728 | tf_op jit(solution)/shard_map/all_gather | solution.py:134
  7.9 394.0 %all-gather.19.cloned.1.call-start = ((), (), s32[]{:S(2)}) async-start(), calls=%async_computation.1 | async-start | bytes 2641920 | tf_op jit(solution)/shard_map/all_gather | solution.py:136
  8.7 593.0 %all-gather.21.cloned.1.call-start = ((), (), s32[]{:S(2)}) async-start(), calls=%async_computation.2 | async-start | bytes 4755456 | tf_op jit(solution)/shard_map/all_gather | solution.py:131
  9.4 795.3 %all-gather.23.cloned.1.call-start = ((), (), s32[]{:S(2)}) async-start(), calls=%async_computation.3 | async-start | bytes 7925760 | tf_op jit(solution)/shard_map/all_gather | solution.py:133
  10.0 1007.7 %all-gather.25.cloned.1.call-start = ((), (), s32[]{:S(2)}) async-start(), calls=%async_computation.4 | async-start | bytes 15851520 | tf_op jit(solution)/shard_map/all_gather | solution.py:137
  10.6 1251.2 %all-gather.27.cloned.1.call-start = ((), (), s32[]{:S(2)}) async-start(), calls=%async_computation.5 | async-start | bytes 39628800 | tf_op jit(solution)/shard_map/all_gather | solution.py:190
  11.1 1494.3 %all-gather.29.cloned.1.call-start = ((), (), s32[]{:S(2)}) async-start(), calls=%async_computation.6 | async-start | bytes 39628800 | tf_op jit(solution)/shard_map/all_gather | solution.py:191
  11.9 1733.1 %all-gather.31.cloned.1.call-start = ((), (), s32[]{:S(2)}) async-start(), calls=%async_computation.7 | async-start | bytes 36986880 | tf_op jit(solution)/shard_map/all_gather | solution.py:192
  12.6 4315.9 %all-reduce.27.cloned.1.call-start = ((), (), s32[]{:S(2)}) async-start(), calls=%async_computation.8 | async-start | bytes 131072000
  1825.7 2504.8 %all-reduce.29.cloned.1.call-start = ((), (), s32[]{:S(2)}) async-start(), calls=%async_computation.9 | async-start | bytes 149422080
  2719.7 855.0 %collective-permute-start.62 = (f32[24,2560]{1,0:T(8,128)S(1)}, f32[24,2560]{1,0:T(8,128)S(1)}, u32[]{:S(2)}, u32[]{:S(2)}) collective-permute-start(f32[24,2560]{1,0:T(8,128)S(1)} %copy-done.36), channel_id=1, source_target_pairs={{0,9},{1,10},{2,11},{3,12},{4,13},{5,14},{6,15},{7,16},{8,17},{9,1... | collective-permute-start | bytes 737288
  2723.8 852.8 %collective-permute-start.61 = (f32[24,2560]{1,0:T(8,128)S(1)}, f32[24,2560]{1,0:T(8,128)}, u32[]{:S(2)}, u32[]{:S(2)}) collective-permute-start(f32[24,2560]{1,0:T(8,128)S(1)} %copy-done.36), channel_id=1, source_target_pairs={{0,8},{1,9},{2,10},{3,11},{4,12},{5,13},{6,14},{7,15},{8,16},{9,17... | collective-permute-start | bytes 737288
  2726.2 877.4 %collective-permute-start.60 = (f32[24,2560]{1,0:T(8,128)S(1)}, f32[24,2560]{1,0:T(8,128)}, u32[]{:S(2)}, u32[]{:S(2)}) collective-permute-start(f32[24,2560]{1,0:T(8,128)S(1)} %copy-done.36), channel_id=1, source_target_pairs={{0,7},{1,8},{2,9},{3,10},{4,11},{5,12},{6,13},{7,14},{8,15},{9,16}... | collective-permute-start | bytes 737288
  2729.2 883.8 %collective-permute-start.59 = (f32[24,2560]{1,0:T(8,128)S(1)}, f32[24,2560]{1,0:T(8,128)}, u32[]{:S(2)}, u32[]{:S(2)}) collective-permute-start(f32[24,2560]{1,0:T(8,128)S(1)} %copy-done.36), channel_id=1, source_target_pairs={{0,6},{1,7},{2,8},{3,9},{4,10},{5,11},{6,12},{7,13},{8,14},{9,15},... | collective-permute-start | bytes 737288
  2732.8 897.2 %collective-permute-start.58 = (f32[24,2560]{1,0:T(8,128)S(1)}, f32[24,2560]{1,0:T(8,128)}, u32[]{:S(2)}, u32[]{:S(2)}) collective-permute-start(f32[24,2560]{1,0:T(8,128)S(1)} %copy-done.36), channel_id=1, source_target_pairs={{0,5},{1,6},{2,7},{3,8},{4,9},{5,10},{6,11},{7,12},{8,13},{9,14},{... | collective-permute-start | bytes 737288
  3574.7 169.0 %collective-permute-start.102 = (f32[64,2560]{1,0:T(8,128)S(1)}, f32[64,2560]{1,0:T(8,128)S(1)}, u32[]{:S(2)}, u32[]{:S(2)}) collective-permute-start(f32[64,2560]{1,0:T(8,128)S(1)} %fusion.3), channel_id=1, source_target_pairs={{0,27},{1,28},{2,29},{3,30},{4,31},{5,32},{6,33},{7,34},{8,35},{9,... | collective-permute-start | bytes 1966088
  3576.6 169.0 %collective-permute-start.101 = (f32[64,2560]{1,0:T(8,128)S(1)}, f32[64,2560]{1,0:T(8,128)S(1)}, u32[]{:S(2)}, u32[]{:S(2)}) collective-permute-start(f32[64,2560]{1,0:T(8,128)S(1)} %fusion.3), channel_id=1, source_target_pairs={{0,26},{1,27},{2,28},{3,29},{4,30},{5,31},{6,32},{7,33},{8,34},{9,... | collective-permute-start | bytes 1966088
  3603.7 138.0 %collective-permute-start.103 = (f32[50,2560]{1,0:T(8,128)S(1)}, f32[50,2560]{1,0:T(8,128)S(1)}, u32[]{:S(2)}, u32[]{:S(2)}) collective-permute-start(f32[50,2560]{1,0:T(8,128)S(1)} %slice.92), channel_id=1, source_target_pairs={{0,28},{1,29},{2,30},{3,31},{4,32},{5,33},{6,34},{7,35},{8,36},{9,... | collective-permute-start | bytes 1536008
  3747.7 117.3 %collective-permute-start.95 = (f32[64,2560]{1,0:T(8,128)S(1)}, f32[64,2560]{1,0:T(8,128)}, u32[]{:S(2)}, u32[]{:S(2)}) collective-permute-start(f32[64,2560]{1,0:T(8,128)S(1)} %fusion.3), channel_id=1, source_target_pairs={{0,20},{1,21},{2,22},{3,23},{4,24},{5,25},{6,26},{7,27},{8,28},{9,... | collective-permute-start | bytes 1966088
  3864.9 205.9 %collective-permute-start.90 = (f32[64,2560]{1,0:T(8,128)S(1)}, f32[64,2560]{1,0:T(8,128)}, u32[]{:S(2)}, u32[]{:S(2)}) collective-permute-start(f32[64,2560]{1,0:T(8,128)S(1)} %fusion.3), channel_id=1, source_target_pairs={{0,15},{1,16},{2,17},{3,18},{4,19},{5,20},{6,21},{7,22},{8,23},{9,... | collective-permute-start | bytes 1966088
  3880.6 195.9 %collective-permute-start.89 = (f32[64,2560]{1,0:T(8,128)S(1)}, f32[64,2560]{1,0:T(8,128)}, u32[]{:S(2)}, u32[]{:S(2)}) collective-permute-start(f32[64,2560]{1,0:T(8,128)S(1)} %fusion.3), channel_id=1, source_target_pairs={{0,14},{1,15},{2,16},{3,17},{4,18},{5,19},{6,20},{7,21},{8,22},{9,... | collective-permute-start | bytes 1966088
  3905.1 174.5 %collective-permute-start.88 = (f32[64,2560]{1,0:T(8,128)S(1)}, f32[64,2560]{1,0:T(8,128)}, u32[]{:S(2)}, u32[]{:S(2)}) collective-permute-start(f32[64,2560]{1,0:T(8,128)S(1)} %fusion.3), channel_id=1, source_target_pairs={{0,13},{1,14},{2,15},{3,16},{4,17},{5,18},{6,19},{7,20},{8,21},{9,... | collective-permute-start | bytes 1966088
  3908.2 174.2 %collective-permute-start.87 = (f32[64,2560]{1,0:T(8,128)S(1)}, f32[64,2560]{1,0:T(8,128)}, u32[]{:S(2)}, u32[]{:S(2)}) collective-permute-start(f32[64,2560]{1,0:T(8,128)S(1)} %fusion.3), channel_id=1, source_target_pairs={{0,12},{1,13},{2,14},{3,15},{4,16},{5,17},{6,18},{7,19},{8,20},{9,... | collective-permute-start | bytes 1966088
  3911.7 172.9 %collective-permute-start.86 = (f32[64,2560]{1,0:T(8,128)S(1)}, f32[64,2560]{1,0:T(8,128)}, u32[]{:S(2)}, u32[]{:S(2)}) collective-permute-start(f32[64,2560]{1,0:T(8,128)S(1)} %fusion.3), channel_id=1, source_target_pairs={{0,11},{1,12},{2,13},{3,14},{4,15},{5,16},{6,17},{7,18},{8,19},{9,... | collective-permute-start | bytes 1966088
  (244 other events, 15814.6 us)
Sparse Core Ops, SparseCore 0:
  9.7 195.6 all-gather.16
  207.1 194.6 all-gather.18
  403.6 198.0 all-gather.20
  603.2 201.3 all-gather.22
  806.2 211.4 all-gather.24
  1019.3 242.3 all-gather.26
  1263.4 241.9 all-gather.28
  1507.1 237.8 all-gather.30
  1825.8 861.5 all-reduce.26
  2693.7 739.7 all-reduce.28
where the time goes:
time: 4360 us; the launch traced here: 4340 us
  waiting for transfers between devices  1520 us (35%)
  blocking collectives  1420 us (33%)
  starting transfers between devices  716 us (16%)
  local copies, waits for them, and re-layouts  417 us (10%)
  matrix products  248 us (6%)
    unnamed x4, blocking collectives  1420 us
    unnamed x106, starting transfers between devices  716 us
    unnamed x344, local copies, waits for them, and re-layouts  411 us
    all_gather x1, waiting for transfers between devices, on_device(): lax.all_gather(gate_weight, ('group', 'replica'), axis=0, tiled=True)  218 us
    all_gather x1, waiting for transfers between devices, on_device(): lax.all_gather(up_weight, ('group', 'replica'), axis=0, tiled=True)  196 us
    all_gather x1, waiting for transfers between devices, on_device(): lax.all_gather(output_weight, ('group', 'replica'), axis=0, tiled=True)  194 us
    all_gather x1, waiting for transfers between devices, on_device(): lax.all_gather(query_up, ('group', 'replica'), axis=0, tiled=True)  193 us
    all_gather x1, waiting for transfers between devices, on_device(): lax.all_gather(latent_up, ('group', 'replica'), axis=0, tiled=True)  192 us
  transfers between devices with their start and end apart: 114, of which 13 were waited for; matrix products, arithmetic and copies ran while one was open for 42% of the time, Pallas kernels for 0%

commit v1 on v0

v1 whole, which is shorter than its diff:
```python
import functools
import math

import jax
import jax.numpy as jnp
import numpy as np
from jax import lax
from jax.experimental import pallas as pl
from jax.experimental.pallas import tpu as pltpu
from jax.sharding import Mesh
from jax.sharding import PartitionSpec as P

D = 2560
QR = 768
KVR = 256
HEADS = 40
NOPE = 64
ROPE = 32
VDIM = 64
FF = 6400
SEQ_LEN = 128
EPS = 1e-05
RESIDUAL = 1.4 / math.sqrt(62.0)
NEGATIVE = -1e30
SCALE = (NOPE + ROPE) ** (-0.5)

AXES = ("zh", "y", "zl", "x", "c")
SIZES = (2, 4, 2, 4, 2)
RING = ("zh", "zl")
TEAM = ("zh", "zl", "c")
SHARDS = ("y", "x")
NTEAM = 8
NSHARD = 16
LAT = 1152
MY_HEADS = HEADS // NTEAM
WIDE = MY_HEADS * 128
PADDED_FF = 896
PADDED_IN = 384

bf16 = jnp.bfloat16
f32 = jnp.float32


def dot(a, b):
    return jnp.dot(a, b, preferred_element_type=f32)


def dot_t(a, b):
    return lax.dot_general(a, b, (((1,), (1,)), ((), ())), preferred_element_type=f32)


def t_dot(a, b):
    return lax.dot_general(a, b, (((0,), (0,)), ((), ())), preferred_element_type=f32)


def up(block):
    return lax.ppermute(block, RING, [(i, (i + 1) % 4) for i in range(4)])


def down(block):
    return lax.ppermute(block, RING, [(i, (i + 3) % 4) for i in range(4)])


def across(block):
    return lax.ppermute(block, "c", [(0, 1), (1, 0)])


def opposite(block):
    pairs = [(2 * z + c, 2 * ((z + (1, 3)[c]) % 4) + c) for z in range(4) for c in range(2)]
    return lax.ppermute(block, TEAM, pairs)


def pick_kernel(core_ref, zero_ref, one_ref, out_ref):
    @pl.when(core_ref[0] == 0)
    def _():
        out_ref[...] = zero_ref[...]

    @pl.when(core_ref[0] != 0)
    def _():
        out_ref[...] = one_ref[...]


def team_near(own):
    return [own, across(own), down(own), None, None, None, up(own), None]


def team_far(blocks, early=(), later=()):
    core = lax.axis_index("c").astype(jnp.int32).reshape(1)
    above, below = blocks[2], blocks[6]
    (mine,) = call(
        pick_kernel, [(above.shape, bf16)], core, below, above, scalars=True, early=early
    )
    far = opposite(mine)
    above, below = gate(above, mine), gate(below, mine)
    blocks = [*blocks[:2], above, across(above), None, None, below, across(below)]
    if later:
        blocks_later = later(blocks)
        far = gate(far, jax.tree.leaves(blocks_later)[0])
        blocks[4:6] = far, across(far)
        return blocks, blocks_later
    blocks[4:6] = far, across(far)
    return blocks


def beyond(block):
    return lax.ppermute(block, RING, [(i, (i + 2) % 4) for i in range(4)])


def team_gather(own, *early):
    above, far, below = down(own), beyond(own), up(own)
    if early:
        above, far, below = gates([above, far, below], *early)
    return [own, across(own), above, across(above), far, across(far), below, across(below)]


def chip_sum(one, two):
    return (one.astype(f32) + across(two).astype(f32)).astype(bf16)


def team_sums(pairs):
    return [chip_sum(*pair) for pair in pairs]


def team_scatter(own, sums):
    above, far, below = sums
    return own[0], across(own[1]), up(above), beyond(far), down(below)


def ring_near(above, below, passing):
    first = (lax.axis_index("c") == 0).astype(f32)
    passed, passing = passing, passing.astype(f32)
    above = above[0].astype(f32) + across(above[1]).astype(f32) + first * passing
    below = below[0].astype(f32) + across(gate(below[1], passed)).astype(f32) + (1.0 - first) * passing
    return above.astype(bf16), below.astype(bf16)


def ring_last(own, above, below):
    above, below = up(above), down(below)
    return own[0], across(gate(own[1], above, below)), above, below


def place():
    return lax.axis_index(RING), lax.axis_index("c")


def absolute_places():
    z, c = place()
    y, x = lax.axis_index("y"), lax.axis_index("x")
    team = [(z + dz) % 4 * 2 + (c + dc) % 2 for dz in range(4) for dc in range(2)]
    shards = [(yy - y + 4) % 4 * 4 + (xx - x + 4) % 4 for yy in range(4) for xx in range(4)]
    owners = [(y + dy) % 4 * 4 + (x + dx) % 4 for dy in range(4) for dx in range(4)]
    return jnp.stack(team + shards + owners).astype(jnp.int32)


def team_exchange(blocks):
    return lax.all_to_all(blocks, TEAM, 0, 0, tiled=True)


def owner_pairs():
    pairs = []
    for zh in range(2):
        for y in range(4):
            for zl in range(2):
                for x in range(4):
                    for c in range(2):
                        source = zh * 64 + y * 16 + zl * 8 + x * 2 + c
                        yy, xx = zl * 2 + x // 2, x % 2 * 2 + c
                        target = zh * 64 + yy * 16 + (y // 2) * 8 + xx * 2 + y % 2
                        pairs.append((source, target))
    return pairs


def to_slices(block):
    return lax.ppermute(block, AXES, owner_pairs())


def to_owners(block):
    return lax.ppermute(block, AXES, [(b, a) for a, b in owner_pairs()])


def shard_gather(block):
    return lax.all_gather(block, SHARDS, axis=0, tiled=False)


def shard_scatter(blocks):
    return lax.psum_scatter(blocks, SHARDS, scatter_dimension=0, tiled=False)


def shard_spread(block, *early):
    def along(axis, rows):
        return [rows] + [
            lax.ppermute(rows, axis, [(i, (i - d) % 4) for i in range(4)]) for d in (1, 2, 3)
        ]

    return along("y", gate(jnp.concatenate(along("x", block), axis=0), *early))


def collect_step(axis, parts, steps):
    return sum(
        lax.ppermute(parts[d], axis, [(i, (i + d) % 4) for i in range(4)]).astype(f32) for d in steps
    )


def shard_collect(slabs, *early):
    rows = (slabs[0].astype(f32) + collect_step("y", slabs, (1, 2, 3))).astype(bf16)
    rows = gate(rows, *early)
    return rows[0].astype(f32) + collect_step("x", rows, (1, 2, 3))


def shard_sum(blocks):
    return jnp.sum(lax.all_to_all(blocks, SHARDS, 0, 0, tiled=True).astype(f32), axis=0)


def gates(late, *early):
    return pl.pallas_call(
        lambda *refs: None,
        in_specs=[pl.BlockSpec(memory_space=pl.ANY)] * (len(late) + len(early)),
        out_specs=[pl.BlockSpec(memory_space=pl.ANY)] * len(late),
        out_shape=[jax.ShapeDtypeStruct(one.shape, one.dtype) for one in late],
        input_output_aliases={i: i for i in range(len(late))},
        cost_estimate=pl.CostEstimate(flops=0, bytes_accessed=0, transcendentals=0),
    )(*late, *early)


def gate(late, *early):
    return gates([late], *early)[0]


def selection(rows, cols, pairs):
    matrix = np.zeros((rows, cols), np.float32)
    for row, col, value in pairs:
        matrix[row, col] = value
    return jnp.asarray(matrix.astype(jnp.bfloat16))


def row_order(quarters):
    pairs = []
    for new in range(1024):
        block, j = divmod(new, 6) if new < QR else divmod(new - QR, 2)
        j = j if new < QR else 6 + j
        zh, y, zl, x, c = block // 64, block // 16 % 4, block // 8 % 2, block // 2 % 4, block % 2
        old = ((((y * 4 + x) * 2 + zh) * 2 + zl) * 2 + c) * 8 + j
        pairs.append((new, old % 4 * 256 + old // 4 if quarters else old, 1.0))
    return selection(1024, 1024, pairs)


def head_rows():
    rows = range(MY_HEADS * VDIM)
    return selection(
        WIDE, PADDED_IN, [(r // VDIM * 128 + NOPE + r % VDIM, r // 20 * 24 + r % 20, 1.0) for r in rows]
    )


def spread():
    pairs = []
    for new in range(WIDE):
        head, lane = divmod(new, 128)
        j = lane - 96
        if j < 0:
            pairs.append((head * 96 + lane, new, 1.0))
        else:
            pairs.append((head * 96 + 64 + (j + 16) % 32, new, -1.0 if j < 16 else 1.0))
    return selection(WIDE, WIDE, pairs)


def rope_keys():
    lanes = [lane for lane in range(WIDE) if lane % 128 >= NOPE]
    return selection(128, WIDE, [(lane % 32, lane, 1.0) for lane in lanes])


GATHERED = [((zh * 4 + y) * 2 + zl) * 4 + x for y in range(4) for x in range(4) for zh in range(2) for zl in range(2)]
OWNED = [GATHERED.index(i) for i in range(64)]


def reorder(rows, order):
    return jnp.concatenate([rows[:, 40 * i : 40 * i + 40] for i in order], axis=1)


def call(kernel, outs, *operands, flops=0, scalars=False, scratch=(), limit=60, early=(), left=0):
    count, skipped = len(operands), len(operands) + len(early)
    spaces = [pl.BlockSpec()] * (count - left)
    spaces += [pl.BlockSpec(memory_space=pl.ANY)] * (left + len(early))
    if scalars:
        spaces[0] = pl.BlockSpec(memory_space=pltpu.SMEM)
    outs = [jax.ShapeDtypeStruct(*out) for out in outs]

    def body(*refs):
        kernel(*refs[:count], *refs[skipped:])

    moved = sum(one.size * one.dtype.itemsize for one in (*operands, *outs))
    return pl.pallas_call(
        body,
        in_specs=spaces,
        out_shape=outs,
        scratch_shapes=list(scratch),
        compiler_params=pltpu.CompilerParams(vmem_limit_bytes=limit * 2**20),
        cost_estimate=pl.CostEstimate(flops=int(flops), bytes_accessed=moved, transcendentals=0),
    )(*operands, *early)


def total(refs):
    return sum(ref[...].astype(f32) for ref in refs)


HIDDEN_SHARDS = [(t, i) for t in range(NTEAM) for i in range(NSHARD)]
UNIT_ROWS = 3 * SEQ_LEN
PACKED_ROWS = UNIT_ROWS + 14 * 24


def entry_kernel(tokens_ref, gate_ref, upper_ref, gain_ref, sent_ref):
    value = tokens_ref[...].astype(f32)
    unit = value * inverse_rms(value)
    gap = jnp.zeros((SEQ_LEN, 4), f32)
    weights = [ref[...].astype(f32) * gain_ref[...] for ref in (gate_ref, upper_ref)]
    wide_gap, low_gap = jnp.zeros((20, 6), f32), jnp.zeros((4, 2 * PADDED_FF), f32)
    for t in range(NTEAM):
        zh, zl, c = t // 4, t // 2 % 2, t % 2
        columns = []
        for y in range(4):
            for x in range(4):
                at = 20 * ((((zh * 4 + y) * 2 + zl) * 4 + x) * 2 + c)
                columns += [unit[:, at : at + 20], gap]
        mine = jnp.concatenate(columns, axis=1).astype(bf16)
        for k in range(3):
            sent_ref[t, SEQ_LEN * k : SEQ_LEN * (k + 1), :] = mine[:, 128 * k : 128 * (k + 1)]
        columns = []
        for weight in weights:
            for i in range(NSHARD):
                at = 800 * t + 50 * i
                columns += [weight[:, at : at + 50], wide_gap]
        mine = jnp.concatenate([jnp.concatenate(columns, axis=1), low_gap], axis=0)
        mine = jnp.concatenate([mine[:, 128 * k : 128 * (k + 1)] for k in range(14)], axis=0)
        sent_ref[t, UNIT_ROWS:, :] = mine.astype(bf16)


def unit_of(received_ref, t):
    return jnp.concatenate(
        [received_ref[t, SEQ_LEN * k : SEQ_LEN * (k + 1), :] for k in range(3)], axis=1
    )


def wide_kernel(received_ref, out_ref):
    rows = []
    for t in range(NTEAM):
        mine = received_ref[t, UNIT_ROWS:, :].astype(f32)
        rows.append(jnp.concatenate([mine[24 * k : 24 * k + 20] for k in range(14)], axis=1))
    out_ref[...] = jnp.concatenate(rows, axis=0).astype(bf16)


def wide_back_kernel(received_ref, gate_ref, upper_ref, gain_ref, gate_out, upper_out, gain_out):
    gain_grad = jnp.zeros((20, 1), f32)
    for weight_ref, out_ref, base in ((gate_ref, gate_out, 0), (upper_ref, upper_out, PADDED_FF)):
        received = [received_ref[t].astype(f32) for t in range(NTEAM)]
        grad = jnp.concatenate(
            [received[t][:, base + 56 * i : base + 56 * i + 50] for t, i in HIDDEN_SHARDS], axis=1
        )
        gain_grad += jnp.sum(grad * weight_ref[...].astype(f32), axis=1, keepdims=True)
        out_ref[...] = gain_ref[...] * grad
    gain_out[...] = gain_grad


def latent_kernel(places_ref, units_ref, *refs):
    downs_refs, outs, downs_ref, held = refs[:4], refs[4:12], refs[12], refs[13]
    for dy in range(4):
        slab = downs_refs[dy][...].astype(f32)
        for dx in range(4):
            held[4 * dy + dx] = slab[24 * dx : 24 * dx + 24]
    downs = jnp.concatenate([held[places_ref[NTEAM + i]] for i in range(NSHARD)], axis=0).astype(bf16)
    downs_ref[...] = downs
    for i in range(NTEAM):
        outs[i][...] = dot(unit_of(units_ref, places_ref[i]), downs).astype(bf16)


def latent_back_kernel(places_ref, units_ref, downs_ref, *refs):
    grad_refs, slabs, unit_grad_ref, held = refs[:8], refs[8:12], refs[12], refs[13]
    units = jnp.concatenate([unit_of(units_ref, places_ref[i]) for i in range(NTEAM)], axis=0)
    grads = jnp.concatenate([ref[...] for ref in grad_refs], axis=0)
    rows = t_dot(units, grads)
    for i in range(NSHARD):
        held[i] = rows[24 * i : 24 * i + 24]
    for dy in range(4):
        for dx in range(4):
            slabs[dy][dx] = held[places_ref[NTEAM + NSHARD + 4 * dy + dx]].astype(bf16)
    downs = downs_ref[...]
    for i in range(NTEAM):
        unit_grad_ref[places_ref[i]] = dot_t(grad_refs[i][...], downs).astype(bf16)


def swapped(rope):
    return jnp.concatenate([-rope[:, 16:32], rope[:, :16], rope[:, 32:]], axis=1)


def packing_kernel(*refs):
    cosine_ref, sine_ref, latent_ref, packed_ref = refs[5:]
    latent = total(refs[:5])
    latent_ref[...] = latent
    query, part, rope = latent[:, :QR], latent[:, QR : QR + KVR], latent[:, QR + KVR :]
    packed_ref[:, :QR] = (query * inverse_rms(query)).astype(bf16)
    packed_ref[:, QR : QR + KVR] = (part * inverse_rms(part)).astype(bf16)
    packed_ref[:, QR + KVR :] = (rope * cosine_ref[...] + swapped(rope) * sine_ref[...]).astype(bf16)


def packing_back_kernel(*refs):
    latent_ref, cosine_ref, sine_ref, out_ref = refs[5:]
    grad = total(refs[:5])
    latent = latent_ref[...]
    for at in (slice(0, QR), slice(QR, QR + KVR)):
        value = latent[:, at]
        out_ref[:, at] = norm_back(value, inverse_rms(value), grad[:, at]).astype(bf16)
    rope = grad[:, QR + KVR :]
    out_ref[:, QR + KVR :] = (rope * cosine_ref[...] - swapped(rope) * sine_ref[...]).astype(bf16)


def scale_kernel(cotangent_ref, out_ref):
    out_ref[...] = (RESIDUAL * cotangent_ref[...].astype(f32)).astype(bf16)


def block_out_kernel(*refs):
    *parts, middle_ref, out_ref = refs
    out_ref[...] = (middle_ref[...] + RESIDUAL * total(parts)).astype(bf16)


def middle_kernel(*refs):
    *parts, tokens_ref, middle_ref, unit_ref = refs
    middle = tokens_ref[...].astype(f32) + RESIDUAL * total(parts)
    middle_ref[...] = middle
    unit_ref[...] = reorder(middle * inverse_rms(middle), GATHERED).astype(bf16)


def middle_back_kernel(*refs):
    middle_ref, cotangent_ref, grad_ref, branch_ref = refs[5:]
    scaled = reorder(total(refs[:5]), OWNED)
    middle = middle_ref[...]
    grad = cotangent_ref[...].astype(f32) + norm_back(middle, inverse_rms(middle), scaled)
    grad_ref[...] = grad
    branch_ref[...] = (RESIDUAL * grad).astype(bf16)


def finish_kernel(unit_grad_ref, tokens_ref, middle_grad_ref, out_ref):
    columns = []
    for b in range(128):
        zh, y, zl, x, c = b // 64, b // 16 % 4, b // 8 % 2, b // 2 % 4, b % 2
        at = 24 * (4 * y + x)
        columns.append(unit_grad_ref[zh * 4 + zl * 2 + c].astype(f32)[:, at : at + 20])
    scaled = jnp.concatenate(columns, axis=1)
    value = tokens_ref[...].astype(f32)
    out_ref[...] = middle_grad_ref[...] + norm_back(value, inverse_rms(value), scaled)


FFN_STEPS = 2


def rows_of(refs):
    return jnp.concatenate([ref[...] for ref in refs], axis=0)


def ffn_kernel(pairs, *refs):
    count = 2 * pairs
    ins, backs, refs = refs[:count], refs[count : 2 * count], refs[2 * count :]
    wide_ref, down_ref, outs, (wide, down_rows, wide_sems, down_sem) = refs[0], refs[1], refs[2:-4], refs[-4:]
    step = D // FFN_STEPS
    copies = [
        pltpu.make_async_copy(
            wide_ref.at[pl.ds(k * step, step)], wide.at[pl.ds(k * step, step)], wide_sems.at[k]
        )
        for k in range(FFN_STEPS)
    ]
    last = pltpu.make_async_copy(down_ref, down_rows, down_sem)
    for copy in (*copies, last):
        copy.start()
    entering = rows_of(ins)
    gate_up = jnp.zeros((count * SEQ_LEN, 2 * PADDED_FF), f32)
    for k, copy in enumerate(copies):
        copy.wait()
        gate_up += dot(entering[:, k * step : (k + 1) * step], wide[k * step : (k + 1) * step])
    last.wait()
    hidden_grad = dot_t(rows_of(backs), down_rows[...])
    gate, upper = gate_up[:, :PADDED_FF], gate_up[:, PADDED_FF:]
    sigma = jax.nn.sigmoid(gate)
    swish = gate * sigma
    hidden = (swish * upper).astype(bf16)
    gate_grad = (hidden_grad * upper * (sigma + swish * (1.0 - sigma))).astype(bf16)
    both = jnp.concatenate([gate_grad, (hidden_grad * swish).astype(bf16)], axis=1)
    width = dot_t(both, wide[...]).astype(bf16)
    for i in range(pairs):
        start = 2 * SEQ_LEN * i
        middle, stop = start + SEQ_LEN, start + 2 * SEQ_LEN
        both_ref, hidden_ref, one_ref, two_ref = outs[4 * i : 4 * i + 4]
        both_ref[...], hidden_ref[...] = both[start:stop], hidden[start:stop]
        one_ref[...], two_ref[...] = width[start:middle], width[middle:stop]


def ffn_out_kernel(*refs):
    down_rows = refs[4][...]
    for i in range(4):
        part = dot(refs[i][...], down_rows).astype(bf16)
        refs[5 + 2 * i][...], refs[6 + 2 * i][...] = part[:SEQ_LEN], part[SEQ_LEN:]


def grouped(flat, size):
    return [flat[i : i + size] for i in range(0, len(flat), size)]


def ffn(ins, backs, wide, down_rows, *early):
    pairs, rows, block = len(ins) // 2, 2 * SEQ_LEN, ((SEQ_LEN, D), bf16)
    outs = call(
        functools.partial(ffn_kernel, pairs),
        [((rows, 2 * PADDED_FF), bf16), ((rows, PADDED_FF), bf16), block, block] * pairs,
        *ins, *backs, wide, down_rows,
        flops=2 * pairs * rows * D * 5 * PADDED_FF, early=early, left=2,
        scratch=[
            pltpu.VMEM((D, 2 * PADDED_FF), bf16), pltpu.VMEM((PADDED_FF, D), bf16),
            pltpu.SemaphoreType.DMA((FFN_STEPS,)), pltpu.SemaphoreType.DMA(()),
        ],
    )
    return grouped(outs, 4)


def slices_kernel(slices_ref, rows_ref, heads_ref, spread_ref, tail_ref, wq_ref, wk_ref, wv_ref, wo_ref, down_ref):
    for i in range(NSHARD):
        down_ref[56 * i : 56 * (i + 1), :] = slices_ref[i, 24:80, :]
    out_rows = jnp.concatenate([slices_ref[i, :24, :].astype(f32) for i in range(NSHARD)], axis=0)
    wo_ref[...] = dot(heads_ref[...], out_rows.astype(bf16)).astype(bf16)
    ups = jnp.concatenate(
        [slices_ref[i, 80:, 640 * k : 640 * (k + 1)] for k in range(4) for i in range(NSHARD)], axis=0
    )
    ups = dot(rows_ref[...], ups).astype(bf16)
    wq_ref[...] = dot(ups[:QR], spread_ref[...]).astype(bf16)
    latent = ups[QR:]
    is_key = lax.broadcasted_iota(jnp.int32, latent.shape, 1) % 128 < NOPE
    wv_ref[...] = jnp.where(is_key, jnp.zeros_like(latent), latent)
    wk_ref[:KVR, :] = jnp.where(is_key, latent, jnp.zeros_like(latent))
    wk_ref[KVR:, :] = tail_ref[...]


def heads_grad_kernel(places_ref, *refs):
    attended_refs, grad_refs, (rows_ref, spread_ref) = refs[:4], refs[4:12], refs[12:14]
    wq_refs, wl_refs, slabs, held = refs[14:17], refs[17:20], refs[20:24], refs[24]
    out_rows = t_dot(rows_of(attended_refs), rows_of(grad_refs))
    grad = jnp.concatenate(
        [dot_t(total(wq_refs).astype(bf16), spread_ref[...]).astype(bf16), total(wl_refs).astype(bf16)], axis=0
    )
    rows = t_dot(rows_ref[...], grad)
    for i in range(NSHARD):
        quarters = [rows[256 * k + 16 * i : 256 * k + 16 * i + 16] for k in range(4)]
        held[i, :24, :] = out_rows[24 * i : 24 * i + 24]
        held[i, 24:, :] = jnp.concatenate(quarters, axis=1)
    for dy in range(4):
        for dx in range(4):
            slabs[dy][dx] = held[places_ref[NTEAM + NSHARD + 4 * dy + dx]].astype(bf16)


def angles():
    place_in = lax.broadcasted_iota(jnp.int32, (SEQ_LEN, ROPE // 2), 0).astype(f32)
    freqs = 10000.0 ** (-2.0 * lax.broadcasted_iota(jnp.int32, (SEQ_LEN, ROPE // 2), 1).astype(f32) / ROPE)
    turn = place_in * freqs
    return jnp.cos(turn), jnp.sin(turn)


def mask_and_scale(q, k):
    scores = dot_t(q, k) * SCALE
    rows = lax.broadcasted_iota(jnp.int32, scores.shape, 0)
    cols = lax.broadcasted_iota(jnp.int32, scores.shape, 1)
    return jnp.where(rows >= cols, scores, NEGATIVE)


def softmax(scores):
    expo = jnp.exp(scores - jnp.max(scores, axis=-1, keepdims=True))
    return expo / jnp.sum(expo, axis=-1, keepdims=True)


def head_places(pairs):
    for s in range(2 * pairs):
        for h in range(MY_HEADS):
            yield slice(s * SEQ_LEN, (s + 1) * SEQ_LEN), slice(h * 128, (h + 1) * 128)


def attend_kernel(pairs, *refs):
    count = 2 * pairs
    wq_ref, wk_ref, wv_ref, wo_ref, turn_ref, rows_ref = refs[count : count + 6]
    outs, attended_ref = refs[count + 6 : -1], refs[-1]
    lat = rows_of(refs[:count])
    queries = dot(lat[:, :QR], wq_ref[...])
    keys = dot(lat[:, QR:], wk_ref[...]).astype(bf16)
    values = dot(lat[:, QR : QR + KVR], wv_ref[...]).astype(bf16)
    turn = turn_ref[...]
    for at in head_places(pairs):
        pair, start = divmod(at[0].start, 2 * SEQ_LEN)
        inner = (slice(start, start + SEQ_LEN), at[1])
        q = (queries[at] * turn).astype(bf16)
        probs = softmax(mask_and_scale(q, keys[at])).astype(bf16)
        outs[7 * pair + 3][inner] = q
        outs[7 * pair + 4][inner] = keys[at]
        outs[7 * pair + 5][inner] = values[at]
        outs[7 * pair + 6][inner] = probs
        attended_ref[at] = dot(probs, values[at]).astype(bf16)
    out_rows = dot(attended_ref[...], rows_ref[...]).astype(bf16)
    out = dot(attended_ref[...], wo_ref[...]).astype(bf16)
    for i in range(pairs):
        start = 2 * SEQ_LEN * i
        middle, stop = start + SEQ_LEN, start + 2 * SEQ_LEN
        outs[7 * i][...], outs[7 * i + 1][...] = out[start:middle], out[middle:stop]
        outs[7 * i + 2][...] = out_rows[start:stop]


def attend_back_kernel(pairs, *refs):
    count = 2 * pairs
    lat, grad = rows_of(refs[:count]), rows_of(refs[count : 2 * count])
    refs = refs[2 * count :]
    heads, (wq_ref, wk_ref, wv_ref, wo_ref, turn_ref) = refs[: 4 * pairs], refs[4 * pairs : 4 * pairs + 5]
    refs = refs[4 * pairs + 5 :]
    outs, (wq_grad_ref, wl_grad_ref, q_grad, k_grad, v_grad) = refs[:count], refs[count:]
    attended_grad = dot_t(grad, wo_ref[...]).astype(bf16)
    turn = turn_ref[...] * SCALE
    for at in head_places(pairs):
        pair, start = divmod(at[0].start, 2 * SEQ_LEN)
        inner = (slice(start, start + SEQ_LEN), at[1])
        queries, keys, values, probs_low = (ref[inner] for ref in heads[4 * pair : 4 * pair + 4])
        probs = probs_low.astype(f32)
        probs_grad = dot_t(attended_grad[at], values)
        mean = jnp.sum(probs * probs_grad, axis=-1, keepdims=True)
        scores_grad = (probs * (probs_grad - mean)).astype(bf16)
        q_grad[at] = (dot(scores_grad, keys) * turn).astype(bf16)
        k_grad[at] = (t_dot(scores_grad, queries) * SCALE).astype(bf16)
        v_grad[at] = t_dot(probs_low, attended_grad[at]).astype(bf16)
    lane = lax.broadcasted_iota(jnp.int32, k_grad.shape, 1)
    kv_grad = jnp.where(lane % 128 < NOPE, k_grad[...], v_grad[...])
    key_side = dot_t(k_grad[...], wk_ref[...])
    value_side = dot_t(v_grad[...], wv_ref[...])
    query_side = dot_t(q_grad[...], wq_ref[...])
    for i, out in enumerate(outs):
        at = slice(SEQ_LEN * i, SEQ_LEN * (i + 1))
        out[:, :QR] = query_side[at].astype(bf16)
        out[:, QR : QR + KVR] = (key_side[at, :KVR] + value_side[at]).astype(bf16)
        out[:, QR + KVR :] = key_side[at, KVR:].astype(bf16)
    wq_grad_ref[...] = t_dot(lat[:, :QR], q_grad[...]).astype(bf16)
    wl_grad_ref[...] = t_dot(lat[:, QR : QR + KVR], kv_grad).astype(bf16)


def whole(shape):
    return pl.BlockSpec(shape, lambda i: (0,) * len(shape))


def attend(blocks, *weights, early=()):
    pairs, rows, block = len(blocks) // 2, 2 * SEQ_LEN, ((SEQ_LEN, D), bf16)
    outs = call(
        functools.partial(attend_kernel, pairs),
        [block, block, ((rows, PADDED_IN), bf16), *([((rows, WIDE), bf16)] * 4)] * pairs,
        *blocks, *weights,
        flops=2 * pairs * rows * (QR * WIDE + 640 * WIDE + WIDE * D + 512 * WIDE),
        scratch=[pltpu.VMEM((pairs * rows, WIDE), bf16)], early=early,
    )
    return grouped(outs, 7)


def attend_back(blocks, grads, heads, weights, early=()):
    pairs, rows = len(blocks) // 2, 2 * SEQ_LEN
    *outs, wq_grad, wl_grad = call(
        functools.partial(attend_back_kernel, pairs),
        [*([((SEQ_LEN, LAT), bf16)] * 2 * pairs), ((QR, WIDE), bf16), ((KVR, WIDE), bf16)],
        *blocks, *grads, *(one for head in heads for one in head[3:]), *weights,
        flops=2 * pairs * rows * (2 * QR * WIDE + 900 * WIDE + WIDE * D + 512 * WIDE),
        scratch=[pltpu.VMEM((pairs * rows, WIDE), bf16)] * 3, early=early,
    )
    return grouped(outs, 2), wq_grad, wl_grad


def ffn_grads_kernel(*refs):
    refs = (*refs[:24], refs[-1])
    ins, backs, boths, hiddens, out_ref = refs[:8], refs[8:16], refs[16:20], refs[20:24], refs[24]
    step = pl.program_id(0)
    left = jnp.concatenate([ref[...] for ref in ins], axis=0)
    wide = t_dot(left, jnp.concatenate([ref[...] for ref in boths], axis=0)).astype(bf16)
    for i in range(4):
        out_ref[i, :160, :] = wide[160 * i : 160 * (i + 1)]
    right = jnp.concatenate([ref[...] for ref in backs], axis=0)

    for now in range(4):

        @pl.when(step == now)
        def _():
            at = slice(224 * now, 224 * (now + 1))
            rows = t_dot(jnp.concatenate([ref[:, at] for ref in hiddens], axis=0), right)
            for i in range(4):
                block = rows[56 * i : 56 * (i + 1)]
                rest = [
                    jnp.concatenate(
                        [block[8 * g : 8 * g + 8, 1792 + 256 * k : 2048 + 256 * k] for g in range(7)], axis=1
                    )
                    for k in range(3)
                ]
                out_ref[i, 160:, :] = jnp.concatenate([block[:, :1792], *rest], axis=0).astype(bf16)


def ffn_grads_of(ins, backs, boths, hiddens, *early):
    rows = 2 * SEQ_LEN
    return pl.pallas_call(
        ffn_grads_kernel,
        grid=(4,),
        in_specs=[pl.BlockSpec((SEQ_LEN, 640), lambda i: (0, i))] * 8
        + [whole((SEQ_LEN, D))] * 8
        + [whole((rows, 2 * PADDED_FF))] * 4
        + [whole((rows, PADDED_FF))] * 4
        + [pl.BlockSpec(memory_space=pl.ANY)] * len(early),
        out_specs=pl.BlockSpec((4, 240, 2 * PADDED_FF), lambda i: (i, 0, 0)),
        out_shape=jax.ShapeDtypeStruct((NSHARD, 240, 2 * PADDED_FF), bf16),
        compiler_params=pltpu.CompilerParams(vmem_limit_bytes=60 * 1024 * 1024),
        cost_estimate=pl.CostEstimate(
            flops=2 * 1024 * D * 3 * PADDED_FF, bytes_accessed=36 * 2**20, transcendentals=0
        ),
    )(*ins, *backs, *boths, *hiddens, *early)


def unpack_down(block):
    rest = block[56:].reshape(3, 8, 7, 256).transpose(2, 1, 0, 3).reshape(56, 768)
    return jnp.concatenate([block[:56], rest], axis=1)


def inverse_rms(value):
    return lax.rsqrt(jnp.mean(value * value, axis=-1, keepdims=True) + EPS)


def norm_back(value, factor, scaled):
    return factor * scaled - value * factor**3 * jnp.mean(scaled * value, axis=-1, keepdims=True)


def on_device(
    tokens,
    entry_gain,
    query_down,
    query_gain,
    query_up,
    latent_down,
    latent_gain,
    latent_up,
    output_weight,
    ffn_gain,
    gate_weight,
    up_weight,
    down_weight,
    cotangent,
):
    count = tokens.shape[0]
    gain_0 = entry_gain.astype(f32)[:, None]
    gain_q = query_gain.astype(f32)[:, None]
    gain_l = latent_gain.astype(f32)[:, None]
    gain_1 = ffn_gain.astype(f32)[:, None]
    downs = jnp.concatenate([query_down, latent_down], axis=1).astype(f32)

    places = absolute_places()
    cosine, sine = angles()
    turn = jnp.concatenate([jnp.ones((SEQ_LEN, NOPE), f32), cosine, cosine, sine, sine], axis=1)
    rest = jnp.zeros((SEQ_LEN, 128 - ROPE), f32)
    cosine = jnp.concatenate([cosine, cosine, rest], axis=1)
    sine = jnp.concatenate([sine, sine, rest], axis=1)

    with jax.named_scope("slices"):
        ups = jnp.concatenate(
            [
                jnp.pad(
                    (gain_q * query_up.astype(f32)).astype(bf16).reshape(6, NTEAM, 480),
                    ((0, 0), (0, 0), (0, 160)),
                ),
                (gain_l * latent_up.astype(f32)).astype(bf16).reshape(2, NTEAM, 640),
            ],
            axis=0,
        )
        ups = team_exchange(ups.transpose(1, 0, 2))
        sliced = jnp.concatenate(
            [jnp.pad(output_weight, ((0, 4), (0, 0))), jnp.pad(down_weight, ((0, 6), (0, 0)))]
        )
        sliced = to_slices(sliced)
        slices = shard_gather(jnp.concatenate([sliced, ups.reshape(16, D)], axis=0))
        in_heads = head_rows()
        spread_in = spread()

    with jax.named_scope("entry"):
        my_downs = jnp.pad((gain_0 * downs).astype(bf16), ((0, 4), (0, LAT - 1056)))
        my_downs = shard_spread(my_downs, ups)
        (sent,) = call(
            entry_kernel, [((NTEAM, PACKED_ROWS, 128), bf16)], tokens, gate_weight, up_weight, gain_1, early=(ups,)
        )
        units = team_exchange(sent)
        *latent, my_downs = call(
            latent_kernel,
            [((SEQ_LEN, LAT), bf16)] * NTEAM + [((PADDED_IN, LAT), bf16)],
            places, units, *my_downs,
            flops=2 * 1024 * PADDED_IN * LAT, scalars=True, scratch=[pltpu.VMEM((NSHARD, 24, LAT), f32)],
        )
        (wide,) = call(wide_kernel, [((160, 2 * PADDED_FF), bf16)], units, early=(my_downs,))
        latent = grouped(latent, 2)
        sums = team_sums(latent[1:])
        latent, packed = call(
            packing_kernel,
            [((SEQ_LEN, LAT), f32), ((SEQ_LEN, LAT), bf16)],
            *team_scatter(latent[0], sums), cosine, sine,
        )
        wq, wk, wv, wo, down_rows = call(
            slices_kernel,
            [((QR, WIDE), bf16), ((LAT - QR, WIDE), bf16), ((KVR, WIDE), bf16), ((WIDE, D), bf16),
             ((PADDED_FF, D), bf16)],
            slices, row_order(True), in_heads, spread_in, rope_keys(),
            flops=2 * WIDE * (PADDED_IN * D + 1024 * 1024 + QR * WIDE),
        )
        weights = (wq, wk, wv, wo, turn)
        (back_in,) = call(scale_kernel, [((SEQ_LEN, D), bf16)], cotangent, early=sums)
        back_in = team_near(back_in)
        lat = team_gather(packed, wq, back_in[2], back_in[6])

    with jax.named_scope("ffn_weights"):
        wide = shard_gather(wide)
        wide = wide.reshape(D, 2 * PADDED_FF)

    with jax.named_scope("attention"):
        back_in = team_far(back_in, lat[4:5])
        (far,) = attend(lat[4:6], *weights, in_heads, early=(back_in[2], back_in[6]))
        far_sum = chip_sum(*far[:2])
        above, below = attend([*lat[2:4], *lat[6:]], *weights, in_heads, early=(far_sum,))
        near = ring_near(above[:2], below[:2], opposite(far_sum))
        (own,) = attend(lat[:2], *weights, in_heads, early=(*near, back_in[4]))
        heads = [own, above, far, below]
        middle, middle_unit = call(
            middle_kernel,
            [((SEQ_LEN, D), f32), ((SEQ_LEN, D), bf16)],
            *ring_last(own[:2], *near), tokens,
        )

    with jax.named_scope("ffn"):
        ins = team_near(middle_unit)
        (own,) = ffn(ins[:2], back_in[:2], wide, down_rows)

        def sides(blocks):
            return ffn([*blocks[2:4], *blocks[6:]], [*back_in[2:4], *back_in[6:]], wide, down_rows)

        ins, (above, below) = team_far(ins, own[:1], sides)
        (far,) = ffn(ins[4:6], back_in[4:6], wide, down_rows)
        parts = [own, above, far, below]
        boths, hiddens = ([part[i] for part in parts] for i in range(2))
        ffn_grads = ffn_grads_of(ins, back_in, boths, hiddens)
        scaled_1 = team_scatter(own[2:], team_sums([above[2:], far[2:], below[2:]]))

    with jax.named_scope("middle_back"):
        middle_grad, branch_grad = call(
            middle_back_kernel,
            [((SEQ_LEN, D), f32), ((SEQ_LEN, D), bf16)],
            *scaled_1, middle, cotangent, early=(ffn_grads,),
        )

    with jax.named_scope("attention_back"):
        grads = team_near(branch_grad)
        (own,), *own_sums = attend_back(lat[:2], grads[:2], heads[:1], weights)

        def back_sides(blocks):
            at = (2, 3, 6, 7)
            return attend_back([lat[i] for i in at], [blocks[i] for i in at], heads[1::2], weights)

        ffn_parts = call(
            ffn_out_kernel, [((SEQ_LEN, D), bf16)] * NTEAM, *hiddens, down_rows,
            flops=2 * 1024 * D * PADDED_FF, early=(branch_grad,),
        )
        grads, ((above, below), *side_sums) = team_far(grads, (own[0], ffn_parts[0]), back_sides)
        (far,), *far_sums = attend_back(lat[4:6], grads[4:6], heads[2:3], weights)
        slabs = call(
            heads_grad_kernel, [((4, 40, D), bf16)] * 4,
            places, *(head[2] for head in heads), *grads, row_order(True), spread_in,
            own_sums[0], side_sums[0], far_sums[0], own_sums[1], side_sums[1], far_sums[1],
            flops=2 * WIDE * (QR * WIDE + 1024 * 1024) + 2 * 1024 * PADDED_IN * D, scalars=True,
            scratch=[pltpu.VMEM((NSHARD, 40, D), f32)],
        )
        packed_grad = team_scatter(own, team_sums([above, far, below]))

    with jax.named_scope("latent_back"):
        (latent_grad,) = call(
            packing_back_kernel, [((SEQ_LEN, LAT), bf16)], *packed_grad, latent, cosine, sine, early=slabs[1:2]
        )
        team_grads = team_gather(latent_grad)
        first_step = slabs[0].astype(f32) + collect_step("y", dict(zip((1, 3), gates(slabs[1::2], latent_grad))), (1, 3))
        *downs_slabs, unit_grad = call(
            latent_back_kernel,
            [((4, 24, LAT), bf16)] * 4 + [((NTEAM, SEQ_LEN, PADDED_IN), bf16)],
            places, units, my_downs, *team_grads,
            flops=4 * 1024 * PADDED_IN * LAT, scalars=True, scratch=[pltpu.VMEM((NSHARD, 24, LAT), f32)],
        )
        unit_back = team_exchange(unit_grad)
        with jax.named_scope("block_out"):
            ffn_parts = grouped(gates(ffn_parts, unit_grad), 2)
            ffn_branch = team_scatter(ffn_parts[0], team_sums(ffn_parts[1:]))
        downs_grad = shard_collect(gates(downs_slabs, first_step), unit_back)[:20, :1056]
        entry_gain_grad = jnp.sum(downs_grad * downs, axis=1)
        downs_grad = gain_0 * downs_grad
        (tokens_grad,) = call(
            finish_kernel, [((SEQ_LEN, D), f32)], unit_back, tokens, middle_grad
        )

    with jax.named_scope("ffn_weight_sums"):
        ffn_grads = lax.psum_scatter(
            gate(ffn_grads, branch_grad).reshape(NSHARD * 240, 2 * PADDED_FF),
            SHARDS, scatter_dimension=0, tiled=True,
        )
        wide_grad = team_exchange(gate(ffn_grads[:160].reshape(NTEAM, 20, 2 * PADDED_FF), unit_back))
        gate_weight_grad, up_weight_grad, ffn_gain_grad = call(
            wide_back_kernel,
            [((20, FF), f32), ((20, FF), f32), ((20, 1), f32)],
            wide_grad, gate_weight, up_weight, gain_1,
        )
        ffn_gain_grad = ffn_gain_grad[:, 0]
        down_weight_grad = to_owners(unpack_down(ffn_grads[160:]))[:50].astype(f32)

        (block_out,) = call(
            block_out_kernel, [((SEQ_LEN, D), bf16)], *ffn_branch, middle, early=(wide_grad,)
        )

    with jax.named_scope("ups_sums"):
        heads_grad = first_step + collect_step("y", {2: gate(slabs[2], first_step, unit_grad)}, (2,))
        heads_grad = heads_grad.astype(bf16)
        heads_grad = (heads_grad[0].astype(f32) + collect_step("x", heads_grad, (1, 2, 3))).astype(bf16)
        output_weight_grad = to_owners(heads_grad[:24])[:20].astype(f32)
        ups_grad = team_exchange(gate(heads_grad[24:].reshape(NTEAM, 8, 640), wide_grad))
        ups_grad = ups_grad.transpose(1, 0, 2).astype(f32)
        query_sum = ups_grad[:6, :, :480].reshape(6, NTEAM * 480)
        latent_sum = ups_grad[6:].reshape(2, NTEAM * 640)
        query_gain_grad = jnp.sum(query_sum * query_up.astype(f32), axis=1)
        latent_gain_grad = jnp.sum(latent_sum * latent_up.astype(f32), axis=1)
        query_up_grad = gain_q * query_sum
        latent_up_grad = gain_l * latent_sum

    return (
        block_out,
        tokens_grad,
        entry_gain_grad,
        downs_grad[:, :QR],
        query_gain_grad,
        query_up_grad,
        downs_grad[:, QR:],
        latent_gain_grad,
        latent_up_grad,
        output_weight_grad,
        ffn_gain_grad,
        gate_weight_grad,
        up_weight_grad,
        down_weight_grad,
    )


def solution(mesh):
    apart = Mesh(mesh.devices.reshape(SIZES), AXES)
    two, one = P(AXES, None), P(AXES)
    return jax.shard_map(
        on_device,
        mesh=apart,
        in_specs=(two, one, two, one, two, two, one, two, two, one, two, two, two, two),
        out_specs=(two, two, one, two, one, two, two, one, two, two, one, two, two, two),
        check_vma=False,
    )
```

time: 4360 us -> 541 us (0.12)
  waiting for transfers between devices: 1520 us -> 94.6 us
  blocking collectives: 1420 us -> 10.2 us
  starting transfers between devices: 716 us -> 122 us
  local copies, waits for them, and re-layouts: 417 us -> 34 us
  matrix products: 248 us -> 0 us
  Pallas kernels: 0 us -> 227 us
    all_gather x8 -> x2, waiting for transfers between devices: 1460 us -> 2.87 us  [shard_gather(): return lax.all_gather(block, SHARDS, axis=0, tiled=False)]
    unnamed x4 -> x0, blocking collectives: 1420 us -> none
    unnamed x106 -> x0, starting transfers between devices: 716 us -> none
    unnamed x344 -> x197, local copies, waits for them, and re-layouts: 411 us -> 27.4 us
    dot_general x30 -> x0, matrix products: 248 us -> none  [the longest x8 107 us: outer(): lax.dot_general(left, right, (((0,), (0,)), ((), ())), preferred_element_...]
    pallas_call x0 -> x48, Pallas kernels: none -> 227 us  [the longest x27 202 us: call(): pl.pallas_call(body, in_specs=spaces, out_shape=outs, scratch_shapes=list...]
    ppermute x0 -> x91, starting transfers between devices: none -> 96.8 us  [the longest x40 25.6 us: across(): return lax.ppermute(block, 'c', [(0, 1), (1, 0)])]
    ppermute x0 -> x91, waiting for transfers between devices: none -> 66 us  [the longest x6 16 us: along(): lax.ppermute(rows, axis, [(i, (i - d) % 4) for i in range(4)])]
  transfers between devices with their start and end apart: 114 -> 98, of which waited for: 13 -> 35; matrix products, arithmetic and copies ran while one was open for 42% -> 6% of each run, Pallas kernels for 0% -> 42%
where the time goes in v1:
time: 541 us; the launch traced here: 531 us
  Pallas kernels  227 us (42%)
  starting transfers between devices  122 us (23%)
  waiting for transfers between devices  94.6 us (17%)
  local copies, waits for them, and re-layouts  34 us (6%)
  other arithmetic  28 us (5%)
  between operations  15 us (3%)
  blocking collectives  10.2 us (2%)
    pallas_call x27, Pallas kernels, call(): pl.pallas_call(body, in_specs=spaces, out_shape=outs, scratch_shapes=list...  202 us
    unnamed x197, local copies, waits for them, and re-layouts  27.4 us
    all_to_all x4, waiting for transfers between devices, team_exchange(): return lax.all_to_all(blocks, TEAM, 0, 0, tiled=True)  25.7 us
    ppermute x40, starting transfers between devices, across(): return lax.ppermute(block, 'c', [(0, 1), (1, 0)])  25.6 us
    all_to_all x4, starting transfers between devices, team_exchange(): return lax.all_to_all(blocks, TEAM, 0, 0, tiled=True)  25.2 us
    pallas_call x1, Pallas kernels, ffn_grads_of(): pl.pallas_call(ffn_grads_kernel, grid=(4,), in_specs=[pl.BlockSpec((SEQ_L...  24.9 us
    ppermute x6, waiting for transfers between devices, along(): lax.ppermute(rows, axis, [(i, (i - d) % 4) for i in range(4)])  16 us
    ppermute x10, starting transfers between devices, down(): return lax.ppermute(block, RING, [(i, (i + 3) % 4) for i in range(4)])  14.9 us
  transfers between devices with their start and end apart: 98, of which 35 were waited for; matrix products, arithmetic and copies ran while one was open for 6% of the time, Pallas kernels for 42%

profile of v1, /device:TPU:31, one launch (start us, length us, event | category | flops | bytes accessed | tf_op | source)
XLA Modules:
  0.0 531.2 jit_solution(9254500066632192498)
XLA Ops:
  15.7 10.2 %all_to_all.25.refs_4_.refs_1_ = bf16[8,8,640]{2,1,0:T(8,128)(2,1)S(1)} all-to-all(bf16[8,8,640]{2,1,0:T(8,128)(2,1)S(1)} %fusion.14), channel_id=1, replica_groups=mesh['zh'=2,'y'=4,'zl'=2,'x'=4,'c'=2] {'zh','zl','c'}, dimensions={0} | all-to-all | bytes 163840 | tf_op jit(solution)/shard_map/slices/all_to_all | solution.py:156
  57.1 5.3 %collective-permute-done.4.refs_4_ = bf16[96,1152]{1,0:T(8,128)(2,1)S(1)} collective-permute-done((bf16[96,1152]{1,0:T(8,128)(2,1)}, bf16[96,1152]{1,0:T(8,128)(2,1)S(1)}, u32[]{:S(2)}, u32[]{:S(2)}) %collective-permute-start.4) | collective-permute-done | bytes 221216 | tf_op jit(solution)/shard_map/entry/ppermute | solution.py:192
  83.7 7.0 %collective-permute-done.10.refs_3_ = bf16[128,1152]{1,0:T(8,128)(2,1)S(1)} collective-permute-done((bf16[128,1152]{1,0:T(8,128)(2,1)S(1)}, bf16[128,1152]{1,0:T(8,128)(2,1)S(1)}, u32[]{:S(2)}, u32[]{:S(2)}) %collective-permute-start.10) | collective-permute-done | bytes 294944 | tf_op jit(solution)/shard_map/entry/ppermute | solution.py:106
  101.4 11.5 %entry.12 = (bf16[768,640]{1,0:T(8,128)(2,1)}, bf16[384,640]{1,0:T(8,128)(2,1)}, bf16[256,640]{1,0:T(8,128)(2,1)}, bf16[640,2560]{1,0:T(8,128)(2,1)}, bf16[896,2560]{1,0:T(8,128)(2,1)}) custom-call(bf16[16,96,2560]{2,1,0:T(8,128)(2,1)} %bitcast.81, bf16[1024,1024]{1,0:T(8,128)(2,1)} %constant.275.clone.refs_1_.refs_13_, ...), custom_call_target="tpu_custom_call" | custom-call | flops 3229614080 | bytes 21102592 | tf_op jit(solution)/shard_map/entry/pallas_call | solution.py:291
  112.9 5.1 collective-permute-done.17.refs_2_
  123.3 8.8 %attention.12 = (bf16[128,2560]{1,0:T(8,128)(2,1)}, bf16[128,2560]{1,0:T(8,128)(2,1)}, bf16[256,384]{1,0:T(8,128)(2,1)}, bf16[256,640]{1,0:T(8,128)(2,1)}, bf16[...) custom-call(bf16[128,1152]{1,0:T(8,128)(2,1)} %get-tuple-element.144.refs_3_.refs_0_, ...), custom_call_target="tpu_custom_call" | custom-call | flops 1468006400 | bytes 9043968 | tf_op jit(solution)/shard_map/attention/pallas_call | solution.py:291
  141.8 14.3 %attention.13 = (bf16[128,2560]{1,0:T(8,128)(2,1)}, bf16[128,2560]{1,0:T(8,128)(2,1)}, bf16[256,384]{1,0:T(8,128)(2,1)}, bf16[256,640]{1,0:T(8,128)(2,1)}, bf16[...) custom-call(bf16[128,1152]{1,0:T(8,128)(2,1)} %get-tuple-element.142, ...), custom_call_target="tpu_custom_call" | custom-call | flops 2936012800 | bytes 12451840 | tf_op jit(solution)/shard_map/attention/pallas_call | solution.py:291
  168.8 8.8 %attention.15 = (bf16[128,2560]{1,0:T(8,128)(2,1)}, bf16[128,2560]{1,0:T(8,128)(2,1)}, bf16[256,384]{1,0:T(8,128)(2,1)}, bf16[256,640]{1,0:T(8,128)(2,1)}, bf16[...) custom-call(bf16[128,1152]{1,0:T(8,128)(2,1)} %get-tuple-element.137.refs_0_, ...), custom_call_target="tpu_custom_call" | custom-call | flops 1468006400 | bytes 9043968 | tf_op jit(solution)/shard_map/attention/pallas_call | solution.py:291
  195.1 13.9 %ffn.8 = (bf16[256,1792]{1,0:T(8,128)(2,1)}, bf16[256,896]{1,0:T(8,128)(2,1)}, bf16[128,2560]{1,0:T(8,128)(2,1)}, bf16[128,2560]{1,0:T(8,128)(2,1)}) custom-call(bf16[128,2560]{1,0:T(8,128)(2,1)} %get-tuple-element.153.refs_0_, bf16[128,2560]{1,0:T(8,128)(2,1)} %copy-done.75, bf16[128,2560]{1,0:T(8,128)(2,1)} %entry.13.refs_2_.refs_8_, ...), custom_call_target="tpu_custom_call" | custom-call | flops 5872025600 | bytes 19070976 | tf_op jit(solution)/shard_map/ffn/pallas_call | solution.py:291
  216.6 22.9 %ffn.12 = (bf16[256,1792]{1,0:T(8,128)(2,1)}, bf16[256,896]{1,0:T(8,128)(2,1)}, bf16[128,2560]{1,0:T(8,128)(2,1)}, bf16[128,2560]{1,0:T(8,128)(2,1)}, bf16[256,1...) custom-call(bf16[128,2560]{1,0:T(8,128)(2,1)} %ffn.10.refs_0_.refs_2_, ...), custom_call_target="tpu_custom_call" | custom-call | flops 11744051200 | bytes 24379392 | tf_op jit(solution)/shard_map/ffn/pallas_call | solution.py:291
  245.7 14.0 %ffn.14 = (bf16[256,1792]{1,0:T(8,128)(2,1)}, bf16[256,896]{1,0:T(8,128)(2,1)}, bf16[128,2560]{1,0:T(8,128)(2,1)}, bf16[128,2560]{1,0:T(8,128)(2,1)}) custom-call(bf16[128,2560]{1,0:T(8,128)(2,1)} %ffn.13.refs_0_.refs_4_, bf16[128,2560]{1,0:T(8,128)(2,1)} %collective-permute-done.40.refs_1_.refs_5_, ...), custom_call_target="tpu_custom_call" | custom-call | flops 5872025600 | bytes 19070976 | tf_op jit(solution)/shard_map/ffn/pallas_call | solution.py:291
  265.2 24.9 %ffn.15.refs_7_.refs_0_ = bf16[16,240,1792]{2,1,0:T(8,128)(2,1)} custom-call(bf16[128,2560]{1,0:T(8,128)(2,1)} %get-tuple-element.153.refs_0_, bf16[128,2560]{1,0:T(8,128)(2,1)} %copy-done.75, bf16[128,2560]{1,0:T(8,128)(2,1)} %ffn.10.refs_0_.refs_2_, bf16[128,2560]{1,0:T(8,128)(2,1)} %copy-done.78, bf16[128,2560]{1,0:T(8,128)(2,1)} %ffn.13.refs_0_.refs_4_, ...), custom_call_target="tpu_custom_call" | custom-call | flops 14092861440 | bytes 37748736 | tf_op jit(solution)/shard_map/ffn/pallas_call | solution.py:697
  291.7 5.6 %middle_back.1 = (f32[128,2560]{1,0:T(8,128)}, bf16[128,2560]{1,0:T(8,128)(2,1)}) custom-call(bf16[128,2560]{1,0:T(8,128)(2,1)} %get-tuple-element.162.refs_0_, bf16[128,2560]{1,0:T(8,128)(2,1)} %copy-done.38, bf16[128,2560]{1,0:T(8,128)(2,1)} %copy-done.40, bf16[128,2560]{1,0:T(8,128)(2,1)} %copy-done.42, bf16[128,2560]{1,0:T(8,128)(2,1)} %copy-done.41, ...), custom_call_target="tpu_custom_call" | custom-call | bytes 7208960 | tf_op jit(solution)/shard_map/middle_back/pallas_call | solution.py:291
  303.5 9.5 %attention_back.9 = (bf16[128,2560]{1,0:T(8,128)(2,1)}, bf16[128,2560]{1,0:T(8,128)(2,1)}, bf16[128,2560]{1,0:T(8,128)(2,1)}, bf16[128,2560]{1,0:T(8,128)(2,1)},...) custom-call(bf16[256,896]{1,0:T(8,128)(2,1)} %get-tuple-element.156., ...), custom_call_target="tpu_custom_call" | custom-call | flops 4697620480 | bytes 11665408 | tf_op jit(solution)/shard_map/attention_back/pallas_call | solution.py:291
  313.9 9.3 %attention_back.10 = (bf16[128,1152]{1,0:T(8,128)(2,1)}, bf16[128,1152]{1,0:T(8,128)(2,1)}, bf16[768,640]{1,0:T(8,128)(2,1)}, bf16[256,640]{1,0:T(8,128)(2,1)}) custom-call(bf16[128,1152]{1,0:T(8,128)(2,1)} %get-tuple-element.137.refs_0_, bf16[128,1152]{1,0:T(8,128)(2,1)} %copy-done.29, bf16[128,2560]{1,0:T(8,128)(2,1)} %get-tuple-element.173.refs_5_.refs_2_.refs_1_, ...), custom_call_target="tpu_custom_call" | custom-call | flops 1804861440 | bytes 10256384 | tf_op jit(solution)/shard_map/attention_back/pallas_call | solution.py:291
  331.8 15.1 %attention_back.14 = (bf16[128,1152]{1,0:T(8,128)(2,1)}, bf16[128,1152]{1,0:T(8,128)(2,1)}, bf16[128,1152]{1,0:T(8,128)(2,1)}, bf16[128,1152]{1,0:T(8,128)(2,1)}...) custom-call(bf16[128,1152]{1,0:T(8,128)(2,1)} %get-tuple-element.142.refs_0_, bf16[128,1152]{1,0:T(8,128)(2,1)} %copy-done.79, ...), custom_call_target="tpu_custom_call" | custom-call | flops 3609722880 | bytes 14057472 | tf_op jit(solution)/shard_map/attention_back/pallas_call | solution.py:291
  351.9 9.5 %attention_back.16 = (bf16[128,1152]{1,0:T(8,128)(2,1)}, bf16[128,1152]{1,0:T(8,128)(2,1)}, bf16[768,640]{1,0:T(8,128)(2,1)}, bf16[256,640]{1,0:T(8,128)(2,1)}) custom-call(bf16[128,1152]{1,0:T(8,128)(2,1)} %get-tuple-element.144.refs_3_.refs_0_, bf16[128,1152]{1,0:T(8,128)(2,1)} %copy-done.27, bf16[128,2560]{1,0:T(8,128)(2,1)} %attention_back.15.refs_2_.refs_9_, ...), custom_call_target="tpu_custom_call" | custom-call | flops 1804861440 | bytes 10256384 | tf_op jit(solution)/shard_map/attention_back/pallas_call | solution.py:291
  366.3 11.3 %attention_back.17 = (bf16[4,40,2560]{2,1,0:T(8,128)(2,1)}, bf16[4,40,2560]{2,1,0:T(8,128)(2,1)}, bf16[4,40,2560]{2,1,0:T(8,128)(2,1)}, bf16[4,40,2560]{2,1,0:T(8,128)(2,1)}) custom-call(s32[40]{0:T(128)} %stack.163.refs_0_, bf16[256,384]{1,0:T(8,128)(2,1)} %get-tuple-element.207.refs_1_, bf16[256,384]{1,0:T(8,128)(2,1)} %get-tuple-element.208.refs_2_, ...), custom_call_target="tpu_custom_call" | custom-call | flops 3984588800 | bytes 16154784 | tf_op jit(solution)/shard_map/attention_back/pallas_call | solution.py:291
  387.2 5.8 %collective-permute-done.64.refs_5_ = bf16[128,1152]{1,0:T(8,128)(2,1)S(1)} collective-permute-done((bf16[128,1152]{1,0:T(8,128)(2,1)S(1)}, bf16[128,1152]{1,0:T(8,128)(2,1)S(1)}, u32[]{:S(2)}, u32[]{:S(2)}) %collective-permute-start.64) | collective-permute-done | bytes 294944 | tf_op jit(solution)/shard_map/latent_back/ppermute | solution.py:61
  405.7 6.4 %latent_back.7 = (bf16[4,24,1152]{2,1,0:T(8,128)(2,1)}, bf16[4,24,1152]{2,1,0:T(8,128)(2,1)}, bf16[4,24,1152]{2,1,0:T(8,128)(2,1)}, bf16[4,24,1152]{2,1,0:T(8,128)(2,1)}, bf16[8,128,384]{2,1,0:T(8,128)(2,1)}) custom-call(s32[40]{0:T(128)} %stack.163.refs_0_, bf16[8,720,128]{2,1,0:T(8,128)(2,1)} %copy-done.7, ...), custom_call_target="tpu_custom_call" | custom-call | flops 1811939328 | bytes 6389920 | tf_op jit(solution)/shard_map/latent_back/pallas_call | solution.py:291
  443.8 4.8 collective-permute-done.85
  466.9 8.8 %all-to-all-start.3 = ((bf16[8,20,1792]{2,1,0:T(8,128)(2,1)}), bf16[8,20,1792]{2,1,0:T(8,128)(2,1)S(1)}, u32[]{:S(2)}, u32[]{:S(2)}) async-start(bf16[8,20,1792]{2,1,0:T(8,128)(2,1)} %ffn_weight_sums.5), calls=%async_computation.4 | async-start | bytes 1376256 | tf_op jit(solution)/shard_map/ffn_weight_sums/all_to_all | solution.py:156
  479.0 25.2 %all-to-all-done.3.refs_6_.refs_1_.refs_0_ = bf16[8,20,1792]{2,1,0:T(8,128)(2,1)S(1)} async-done(((bf16[8,20,1792]{2,1,0:T(8,128)(2,1)}), bf16[8,20,1792]{2,1,0:T(8,128)(2,1)S(1)}, u32[]{:S(2)}, u32[]{:S(2)}) %all-to-all-start.3) | async-done | bytes 573472 | tf_op jit(solution)/shard_map/ffn_weight_sums/all_to_all | solution.py:156
  505.1 7.4 %all-to-all-start.4 = ((bf16[8,8,640]{2,1,0:T(8,128)(2,1)}), bf16[8,8,640]{2,1,0:T(8,128)(2,1)S(1)}, u32[]{:S(2)}, u32[]{:S(2)}) async-start(bf16[8,8,640]{2,1,0:T(8,128)(2,1)} %ups_sums.3), calls=%async_computation.5 | async-start | bytes 163840 | tf_op jit(solution)/shard_map/ups_sums/all_to_all | solution.py:156
  (490 shorter events, 250.7 us)
Async XLA Ops:
  7.2 94.2 %all-gather.5.cloned.1.call-start = ((), (), s32[]{:S(2)}) async-start(), calls=%async_computation.7 | async-start | bytes 8355840 | tf_op jit(solution)/shard_map/slices/all_gather | solution.py:182
  32.3 30.1 %all-to-all-start.1 = ((bf16[8,720,128]{2,1,0:T(8,128)(2,1)}), bf16[8,720,128]{2,1,0:T(8,128)(2,1)S(1)}, u32[]{:S(2)}, u32[]{:S(2)}) async-start(bf16[8,720,128]{2,1,0:T(8,128)(2,1)} %entry.8), calls=%async_computation.1 | async-start | bytes 2949120 | tf_op jit(solution)/shard_map/entry/all_to_all | solution.py:156
  36.7 157.5 %all-gather.7.cloned.1.call-start = ((), (), s32[]{:S(2)}) async-start(), calls=%async_computation.8 | async-start | bytes 9748480 | tf_op jit(solution)/shard_map/ffn_weights/all_gather | solution.py:182
  71.3 393.5 %reduce-scatter.2.cloned.1.call-start = ((), (), s32[]{:S(2)}) async-start(), calls=%async_computation.6 | async-start | bytes 14622720 | tf_op jit(solution)/shard_map/ffn_weight_sums/reduce_scatter | solution.py:896
  81.1 36.9 %collective-permute-start.18 = (bf16[128,2560]{1,0:T(8,128)(2,1)}, bf16[128,2560]{1,0:T(8,128)(2,1)S(1)}, u32[]{:S(2)}, u32[]{:S(2)}) collective-permute-start(bf16[128,2560]{1,0:T(8,128)(2,1)} %entry.13.refs_2_.refs_8_), channel_id=1, source_target_pairs={{0,72},{8,0},{64,8},{72,64},{1,73},{9,1},{65,9},{73,65},{2,74},{10... | collective-permute-start | bytes 1966088 | tf_op jit(solution)/shard_map/entry/ppermute | solution.py:61
  81.7 36.2 %collective-permute-start.19 = (bf16[128,2560]{1,0:T(8,128)(2,1)}, bf16[128,2560]{1,0:T(8,128)(2,1)S(1)}, u32[]{:S(2)}, u32[]{:S(2)}) collective-permute-start(bf16[128,2560]{1,0:T(8,128)(2,1)} %entry.13.refs_2_.refs_8_), channel_id=1, source_target_pairs={{0,8},{8,64},{64,72},{72,0},{1,9},{9,65},{65,73},{73,1},{2,10},{10... | collective-permute-start | bytes 1966088 | tf_op jit(solution)/shard_map/entry/ppermute | solution.py:57
  193.4 21.4 %collective-permute-start.37 = (bf16[128,2560]{1,0:T(8,128)(2,1)S(1)}, bf16[128,2560]{1,0:T(8,128)(2,1)}, u32[]{:S(2)}, u32[]{:S(2)}) collective-permute-start(bf16[128,2560]{1,0:T(8,128)(2,1)S(1)} %copy-done.4), channel_id=1, source_target_pairs={{0,1},{1,0},{2,3},{3,2},{4,5},{5,4},{6,7},{7,6},{8,9},{9,8},{10,11... | collective-permute-start | bytes 1966088 | tf_op jit(solution)/shard_map/attention/ppermute | solution.py:65
  213.7 26.8 %collective-permute-start.39 = (bf16[128,2560]{1,0:T(8,128)(2,1)S(1)}, bf16[128,2560]{1,0:T(8,128)(2,1)S(1)}, u32[]{:S(2)}, u32[]{:S(2)}) collective-permute-start(bf16[128,2560]{1,0:T(8,128)(2,1)S(1)} %copy-done.9), channel_id=1, source_target_pairs={{0,8},{1,73},{8,64},{9,1},{64,72},{65,9},{72,0},{73,65},{2,10},{3,... | collective-permute-start | bytes 1966088 | tf_op jit(solution)/shard_map/ffn/ppermute | solution.py:70
  240.1 50.1 %collective-permute-start.42 = (bf16[128,2560]{1,0:T(8,128)(2,1)}, bf16[128,2560]{1,0:T(8,128)(2,1)S(1)}, u32[]{:S(2)}, u32[]{:S(2)}) collective-permute-start(bf16[128,2560]{1,0:T(8,128)(2,1)} %get-tuple-element.163), channel_id=1, source_target_pairs={{0,1},{1,0},{2,3},{3,2},{4,5},{5,4},{6,7},{7,6},{8,9},{9,8},{10,11... | collective-permute-start | bytes 1966088 | tf_op jit(solution)/shard_map/ffn/ppermute | solution.py:65
  244.0 46.2 %collective-permute-start.44 = (bf16[128,2560]{1,0:T(8,128)(2,1)S(1)}, bf16[128,2560]{1,0:T(8,128)(2,1)S(1)}, u32[]{:S(2)}, u32[]{:S(2)}) collective-permute-start(bf16[128,2560]{1,0:T(8,128)(2,1)S(1)} %add_convert_fusion.6), channel_id=1, source_target_pairs={{0,8},{8,64},{64,72},{72,0},{1,9},{9,65},{65,73},{73,1},{2,10},{10... | collective-permute-start | bytes 1966088 | tf_op jit(solution)/shard_map/ffn/ppermute | solution.py:57
  261.2 29.0 %collective-permute-start.48 = (bf16[128,2560]{1,0:T(8,128)(2,1)}, bf16[128,2560]{1,0:T(8,128)(2,1)S(1)}, u32[]{:S(2)}, u32[]{:S(2)}) collective-permute-start(bf16[128,2560]{1,0:T(8,128)(2,1)} %add_convert_fusion.4), channel_id=1, source_target_pairs={{0,72},{8,0},{64,8},{72,64},{1,73},{9,1},{65,9},{73,65},{2,74},{10... | collective-permute-start | bytes 1966088 | tf_op jit(solution)/shard_map/ffn/ppermute | solution.py:61
  263.9 26.3 %collective-permute-start.46 = (bf16[128,2560]{1,0:T(8,128)(2,1)}, bf16[128,2560]{1,0:T(8,128)(2,1)S(1)}, u32[]{:S(2)}, u32[]{:S(2)}) collective-permute-start(bf16[128,2560]{1,0:T(8,128)(2,1)} %add_convert_fusion.5), channel_id=1, source_target_pairs={{0,64},{8,72},{64,0},{72,8},{1,65},{9,73},{65,1},{73,9},{2,66},{10... | collective-permute-start | bytes 1966088 | tf_op jit(solution)/shard_map/ffn/ppermute | solution.py:106
  300.0 23.2 %collective-permute-start.51 = (bf16[128,2560]{1,0:T(8,128)(2,1)S(1)}, bf16[128,2560]{1,0:T(8,128)(2,1)S(1)}, u32[]{:S(2)}, u32[]{:S(2)}) collective-permute-start(bf16[128,2560]{1,0:T(8,128)(2,1)S(1)} %copy-done.12), channel_id=1, source_target_pairs={{0,72},{8,0},{64,8},{72,64},{1,73},{9,1},{65,9},{73,65},{2,74},{10... | collective-permute-start | bytes 1966088 | tf_op jit(solution)/shard_map/attention_back/ppermute | solution.py:61
  348.4 29.3 %collective-permute-start.50 = (bf16[128,1152]{1,0:T(8,128)(2,1)S(1)}, bf16[128,1152]{1,0:T(8,128)(2,1)S(1)}, u32[]{:S(2)}, u32[]{:S(2)}) collective-permute-start(bf16[128,1152]{1,0:T(8,128)(2,1)S(1)} %copy-done.81), channel_id=1, source_target_pairs={{0,1},{1,0},{2,3},{3,2},{4,5},{5,4},{6,7},{7,6},{8,9},{9,8},{10,11... | collective-permute-start | bytes 884744 | tf_op jit(solution)/shard_map/attention_back/ppermute | solution.py:65
  349.0 28.7 %collective-permute-start.56 = (bf16[128,1152]{1,0:T(8,128)(2,1)S(1)}, bf16[128,1152]{1,0:T(8,128)(2,1)S(1)}, u32[]{:S(2)}, u32[]{:S(2)}) collective-permute-start(bf16[128,1152]{1,0:T(8,128)(2,1)S(1)} %add_convert_fusion.10), channel_id=1, source_target_pairs={{0,8},{8,64},{64,72},{72,0},{1,9},{9,65},{65,73},{73,1},{2,10},{10... | collective-permute-start | bytes 884744 | tf_op jit(solution)/shard_map/attention_back/ppermute | solution.py:57
  382.3 30.0 %collective-permute-start.78 = (bf16[4,40,2560]{2,1,0:T(8,128)(2,1)}, bf16[4,40,2560]{2,1,0:T(8,128)(2,1)S(1)}, u32[]{:S(2)}, u32[]{:S(2)}) collective-permute-start(bf16[4,40,2560]{2,1,0:T(8,128)(2,1)} %get-tuple-element.235), channel_id=1, source_target_pairs={{0,48},{16,0},{32,16},{48,32},{1,49},{17,1},{33,17},{49,33},{2,50}... | collective-permute-start | bytes 2457608 | tf_op jit(solution)/shard_map/latent_back/ppermute | solution.py:200
  382.8 29.5 %collective-permute-start.77 = (bf16[4,40,2560]{2,1,0:T(8,128)(2,1)}, bf16[4,40,2560]{2,1,0:T(8,128)(2,1)S(1)}, u32[]{:S(2)}, u32[]{:S(2)}) collective-permute-start(bf16[4,40,2560]{2,1,0:T(8,128)(2,1)} %get-tuple-element.234), channel_id=1, source_target_pairs={{0,16},{16,32},{32,48},{48,0},{1,17},{17,33},{33,49},{49,1},{2,18}... | collective-permute-start | bytes 2457608 | tf_op jit(solution)/shard_map/latent_back/ppermute | solution.py:200
  423.0 94.8 %collective-permute-start.70 = (bf16[128,2560]{1,0:T(8,128)(2,1)S(1)}, bf16[128,2560]{1,0:T(8,128)(2,1)}, u32[]{:S(2)}, u32[]{:S(2)}) collective-permute-start(bf16[128,2560]{1,0:T(8,128)(2,1)S(1)} %copy-done.43), channel_id=1, source_target_pairs={{0,1},{1,0},{2,3},{3,2},{4,5},{5,4},{6,7},{7,6},{8,9},{9,8},{10,11... | collective-permute-start | bytes 1966088 | tf_op jit(solution)/shard_map/latent_back/block_out/ppermute | solution.py:65
  427.8 20.8 %collective-permute-start.85 = (bf16[4,40,2560]{2,1,0:T(8,128)(2,1)}, bf16[4,40,2560]{2,1,0:T(8,128)(2,1)S(1)}, u32[]{:S(2)}, u32[]{:S(2)}) collective-permute-start(bf16[4,40,2560]{2,1,0:T(8,128)(2,1)} %ups_sums.2), channel_id=1, source_target_pairs={{0,32},{16,48},{32,0},{48,16},{1,33},{17,49},{33,1},{49,17},{2,34}... | collective-permute-start | bytes 2457608 | tf_op jit(solution)/shard_map/ups_sums/ppermute | solution.py:200
  432.4 85.5 %collective-permute-start.72 = (bf16[128,2560]{1,0:T(8,128)(2,1)}, bf16[128,2560]{1,0:T(8,128)(2,1)}, u32[]{:S(2)}, u32[]{:S(2)}) collective-permute-start(bf16[128,2560]{1,0:T(8,128)(2,1)} %add_convert_fusion.3), channel_id=1, source_target_pairs={{0,8},{8,64},{64,72},{72,0},{1,9},{9,65},{65,73},{73,1},{2,10},{10... | collective-permute-start | bytes 1966088 | tf_op jit(solution)/shard_map/latent_back/block_out/ppermute | solution.py:57
  456.1 61.7 %collective-permute-start.74 = (bf16[128,2560]{1,0:T(8,128)(2,1)S(1)}, bf16[128,2560]{1,0:T(8,128)(2,1)}, u32[]{:S(2)}, u32[]{:S(2)}) collective-permute-start(bf16[128,2560]{1,0:T(8,128)(2,1)S(1)} %add_convert_fusion.2), channel_id=1, source_target_pairs={{0,64},{8,72},{64,0},{72,8},{1,65},{9,73},{65,1},{73,9},{2,66},{10... | collective-permute-start | bytes 1966088 | tf_op jit(solution)/shard_map/latent_back/block_out/ppermute | solution.py:106
  462.0 55.9 %collective-permute-start.76 = (bf16[128,2560]{1,0:T(8,128)(2,1)}, bf16[128,2560]{1,0:T(8,128)(2,1)}, u32[]{:S(2)}, u32[]{:S(2)}) collective-permute-start(bf16[128,2560]{1,0:T(8,128)(2,1)} %add_convert_fusion.1), channel_id=1, source_target_pairs={{0,72},{8,0},{64,8},{72,64},{1,73},{9,1},{65,9},{73,65},{2,74},{10... | collective-permute-start | bytes 1966088 | tf_op jit(solution)/shard_map/latent_back/block_out/ppermute | solution.py:61
  466.9 37.4 %all-to-all-start.3 = ((bf16[8,20,1792]{2,1,0:T(8,128)(2,1)}), bf16[8,20,1792]{2,1,0:T(8,128)(2,1)S(1)}, u32[]{:S(2)}, u32[]{:S(2)}) async-start(bf16[8,20,1792]{2,1,0:T(8,128)(2,1)} %ffn_weight_sums.5), calls=%async_computation.4 | async-start | bytes 1376256 | tf_op jit(solution)/shard_map/ffn_weight_sums/all_to_all | solution.py:156
  475.7 36.8 %collective-permute-start.90 = (bf16[56,2560]{1,0:T(8,128)(2,1)S(1)}, bf16[56,2560]{1,0:T(8,128)(2,1)S(1)}, u32[]{:S(2)}, u32[]{:S(2)}) collective-permute-start(bf16[56,2560]{1,0:T(8,128)(2,1)S(1)} %pad_maximum_fusion.1), channel_id=1, source_target_pairs={{0,0},{2,1},{4,2},{6,3},{16,4},{18,5},{20,6},{22,7},{32,8},{34,9},... | collective-permute-start | bytes 860168 | tf_op jit(solution)/shard_map/ffn_weight_sums/ppermute | solution.py:178
  (175 other events, 1087.1 us)
Sparse Core Ops, SparseCore 0:
  27.0 74.3 all-gather.4
  104.1 73.9 all-gather.6
  297.4 106.0 reduce-scatter.1
